TPU v7x, 128 devices: a whole 4x4x4 slice. The times are simulated.
128 devices in a mesh: dp: 4 (over y), retr: 32 (over z, x, core).
Axes of the slice: x: 4, y: 4, z: 4, core: 2. Of those that a mesh axis runs over, the one named last changes fastest.
Arguments:
- query: bfloat16 [1024, 64, 2048], P(('dp', 'retr')), may hold values from -20 to 20
- grad_out: bfloat16 [1024, 64, 2048], P(('dp', 'retr')), may hold values from -12 to 12
- keys: bfloat16 [192, 128, 2048], P('retr'), may hold values from -4 to 4
- values: bfloat16 [192, 128, 2048], P('retr'), may hold values from -4 to 4
- owner_list: int32 [1024, 2], P(('dp', 'retr')), may hold values from 0 to 31, as said below
- row_list: int32 [1024, 2], P(('dp', 'retr')), may hold values from 0 to 5
Outputs:
- grad_query: bfloat16 [1024, 64, 2048], P(('dp', 'retr'))
- grad_keys: bfloat16 [192, 128, 2048], P('retr', 'dp')
- grad_values: bfloat16 [192, 128, 2048], P('retr', 'dp')
Inputs may be any that keep to these rules, and one draw needn't show every extreme that they name: `owner_list`: spans lie on devices in blocks of 8; the 16 entries of one block name any one owner at most 1 times, and in every draw some owners are named exactly 1 times by every block. Owners are indices along retr within the span's own dp group.
All inputs are finite; a program needn't handle non-finite values.
Results may differ from a plain program's by a relative error of at most 0.0076.
Values may be sent and summed in bfloat16 or wider, within the bound.
A program may use at most 256 MiB of HBM per device.

v0:
```python
import jax
import jax.numpy as jnp
from jax import lax
from jax.sharding import PartitionSpec as P

HEADS = 16


slots_per_pass = 8


def chosen_rows(onehot, table):
    return jnp.einsum("sr,rtc->stc", onehot, table, preferred_element_type=jnp.float32).astype(
        jnp.bfloat16
    )


def head_split(array, head_count):
    return array.reshape(array.shape[0], array.shape[1], head_count, array.shape[2] // head_count)


def passes_of(array):
    return array.reshape((array.shape[0] // slots_per_pass, slots_per_pass) + array.shape[1:])


def slots_of(array):
    return array.reshape((array.shape[0] * array.shape[1],) + array.shape[2:])


def on_device(query, grad_out, keys, values, owner_list, row_list):
    owners_count = lax.axis_size("retr")
    spans, span_len, width = query.shape
    row_count, key_len, _ = keys.shape
    head_count = HEADS
    scaling = (width // head_count) ** (-0.5)
    entries = 2 * spans
    slot_count = 4 * spans
    capacity = slot_count // owners_count
    owners = owner_list.reshape(entries)
    row_index = row_list.reshape(entries)
    to_owner = (owners[:, None] == jnp.arange(owners_count, dtype=jnp.int32)[None, :]).astype(
        jnp.int32
    )
    earlier = jnp.cumsum(to_owner, axis=0) - to_owner
    position = owners * capacity + jnp.sum(earlier * to_owner, axis=1)
    placing = position[None, :] == jnp.arange(slot_count, dtype=jnp.int32)[:, None]
    by_span = jnp.any(placing.reshape(slot_count, spans, 2), axis=2).astype(jnp.bfloat16)
    row_onehot = (row_index[:, None] == jnp.arange(row_count, dtype=jnp.int32)[None, :]).astype(
        jnp.bfloat16
    )
    slot_rows = jnp.dot(
        placing.astype(jnp.bfloat16), row_onehot, preferred_element_type=jnp.float32
    ).astype(jnp.bfloat16)
    slot_span = (
        jnp.sum(placing.astype(jnp.int32) * jnp.arange(entries, dtype=jnp.int32)[None, :], axis=1)
        // 2
    )
    send_query = jnp.einsum(
        "sc,ctd->std", by_span, query, preferred_element_type=jnp.float32
    ).astype(jnp.bfloat16)
    send_grad = jnp.einsum(
        "sc,ctd->std", by_span, grad_out, preferred_element_type=jnp.float32
    ).astype(jnp.bfloat16)

    def scores_for(query_pass, key_pass):
        return (
            jnp.einsum(
                "sqhd,skhd->shqk",
                head_split(query_pass, head_count),
                head_split(key_pass, head_count),
                preferred_element_type=jnp.float32,
            )
            * scaling
        )

    def dprob_for(grad_pass, value_pass):
        return jnp.einsum(
            "sqhd,skhd->shqk",
            head_split(grad_pass, head_count),
            head_split(value_pass, head_count),
            preferred_element_type=jnp.float32,
        )

    got_query, got_grad, got_rows = (
        lax.all_to_all(send_query, "retr", split_axis=0, concat_axis=0, tiled=True),
        lax.all_to_all(send_grad, "retr", split_axis=0, concat_axis=0, tiled=True),
        lax.all_to_all(slot_rows, "retr", split_axis=0, concat_axis=0, tiled=True),
    )

    def first_pass(pieces):
        query_pass, grad_pass, rows_pass = pieces
        scores = scores_for(query_pass, chosen_rows(rows_pass, keys))
        maxima = jnp.max(scores, axis=-1)
        lifted = jnp.exp(scores - maxima[..., None])
        dprob = dprob_for(grad_pass, chosen_rows(rows_pass, values))
        return (maxima, jnp.sum(lifted, axis=-1), jnp.sum(lifted * dprob, axis=-1))

    maxima, totals, weighted = lax.map(
        first_pass, (passes_of(got_query), passes_of(got_grad), passes_of(got_rows))
    )
    maxima = slots_of(maxima)
    totals = slots_of(totals)
    weighted = slots_of(weighted)
    returned_stats = (
        lax.all_to_all(maxima, "retr", split_axis=0, concat_axis=0, tiled=True),
        lax.all_to_all(totals, "retr", split_axis=0, concat_axis=0, tiled=True),
        lax.all_to_all(weighted, "retr", split_axis=0, concat_axis=0, tiled=True),
    )
    stat_shape = (spans, 2, head_count, span_len)
    maxima_each = jnp.take(returned_stats[0], position, axis=0).reshape(stat_shape)
    totals_each = jnp.take(returned_stats[1], position, axis=0).reshape(stat_shape)
    weighted_each = jnp.take(returned_stats[2], position, axis=0).reshape(stat_shape)
    joint_max = jnp.max(maxima_each, axis=1)
    factor = jnp.exp(maxima_each - joint_max[:, None])
    masses = jnp.sum(factor * totals_each, axis=1)
    log_norm = joint_max + jnp.log(masses)
    deltas = jnp.sum(factor * weighted_each, axis=1) / masses
    slot_norm = jnp.take(log_norm, slot_span, axis=0)
    slot_delta = jnp.take(deltas, slot_span, axis=0)
    arrived_norms = (
        lax.all_to_all(slot_norm, "retr", split_axis=0, concat_axis=0, tiled=True),
        lax.all_to_all(slot_delta, "retr", split_axis=0, concat_axis=0, tiled=True),
    )

    def gradients(carry, pieces):
        key_sum, value_sum = carry
        query_pass, grad_pass, rows_pass, norm_pass, delta_pass = pieces
        key_pass = chosen_rows(rows_pass, keys)
        value_pass = chosen_rows(rows_pass, values)
        query_heads = head_split(query_pass, head_count)
        grad_heads = head_split(grad_pass, head_count)
        key_heads = head_split(key_pass, head_count)
        scores = scores_for(query_pass, key_pass)
        dprob = dprob_for(grad_pass, value_pass)
        chance = jnp.exp(scores - norm_pass[..., None])
        chance_low = chance.astype(jnp.bfloat16)
        dscore = (scaling * chance * (dprob - delta_pass[..., None])).astype(jnp.bfloat16)
        value_terms = jnp.einsum(
            "shqk,sqhd->skhd", chance_low, grad_heads, preferred_element_type=jnp.float32
        ).reshape(slots_per_pass, key_len, width)
        key_terms = jnp.einsum(
            "shqk,sqhd->skhd", dscore, query_heads, preferred_element_type=jnp.float32
        ).reshape(slots_per_pass, key_len, width)
        query_terms = (
            jnp.einsum("shqk,skhd->sqhd", dscore, key_heads, preferred_element_type=jnp.float32)
            .astype(jnp.bfloat16)
            .reshape(slots_per_pass, span_len, width)
        )
        weights = rows_pass.astype(jnp.float32)
        key_sum = key_sum + jnp.einsum(
            "sr,stc->rtc", weights, key_terms, precision=lax.Precision.HIGHEST
        )
        value_sum = value_sum + jnp.einsum(
            "sr,stc->rtc", weights, value_terms, precision=lax.Precision.HIGHEST
        )
        return ((key_sum, value_sum), query_terms)

    zero_rows = jnp.zeros((row_count, key_len, width), jnp.float32)
    (key_sum, value_sum), query_back = lax.scan(
        gradients,
        (zero_rows, zero_rows),
        (
            passes_of(got_query),
            passes_of(got_grad),
            passes_of(got_rows),
            passes_of(arrived_norms[0]),
            passes_of(arrived_norms[1]),
        ),
    )
    returned = lax.all_to_all(slots_of(query_back), "retr", split_axis=0, concat_axis=0, tiled=True)
    halves = jnp.take(returned, position, axis=0).reshape(spans, 2, span_len, width)
    grad_query = (halves[:, 0].astype(jnp.float32) + halves[:, 1].astype(jnp.float32)).astype(
        jnp.bfloat16
    )
    key_part, value_part = (
        lax.psum_scatter(key_sum, "dp", scatter_dimension=1, tiled=True),
        lax.psum_scatter(value_sum, "dp", scatter_dimension=1, tiled=True),
    )
    return (grad_query, key_part.astype(jnp.bfloat16), value_part.astype(jnp.bfloat16))


def solution(mesh):
    return jax.shard_map(
        on_device,
        mesh=mesh,
        in_specs=(
            P(("dp", "retr"), None, None),
            P(("dp", "retr"), None, None),
            P("retr", None, None),
            P("retr", None, None),
            P(("dp", "retr"), None),
            P(("dp", "retr"), None),
        ),
        out_specs=(P(("dp", "retr"), None, None), P("retr", "dp", None), P("retr", "dp", None)),
        check_vma=False,
    )
```

profile of v0, /device:TPU:1, one launch (start us, length us, event | category | flops | bytes accessed | tf_op | source)
XLA Modules:
  0.0 914.5 jit_solution(17840353469584742363)
XLA Ops:
  10.3 9.4 %all-to-all-start = ((bf16[32,1,6]{2,1,0:T(2,128)(2,1)}), bf16[32,1,6]{2,1,0:T(2,128)(2,1)S(1)}, u32[]{:S(2)}, u32[]{:S(2)}) async-start(bf16[32,1,6]{2,1,0:T(2,128)(2,1)} %copy.155), calls=%async_computation | async-start | bytes 32768 | tf_op jit(solution)/shard_map/all_to_all | solution.py:87
  25.3 11.2 %copy.161 = bf16[32,64,2048]{2,1,0:T(8,128)(2,1)} copy(bf16[32,64,2048]{2,0,1:T(8,128)(2,1)} %convolution_convert_fusion) | data formatting | bytes 16777216 | tf_op jit(solution)/shard_map/convert_element_type | solution.py:63
  36.5 8.0 all-to-all-start.2
  49.1 11.2 %copy.159 = bf16[32,64,2048]{2,1,0:T(8,128)(2,1)} copy(bf16[32,64,2048]{2,0,1:T(8,128)(2,1)} %convolution_convert_fusion.1) | data formatting | bytes 16777216 | tf_op jit(solution)/shard_map/convert_element_type | solution.py:60
  60.4 83.5 %all-to-all-done.2 = bf16[32,64,2048]{2,1,0:T(8,128)(2,1)} async-done(((bf16[32,64,2048]{2,1,0:T(8,128)(2,1)}), bf16[32,64,2048]{2,1,0:T(8,128)(2,1)}, u32[]{:S(2)}, u32[]{:S(2)}) %all-to-all-start.2) | async-done | bytes 8388640 | tf_op jit(solution)/shard_map/all_to_all | solution.py:86
  143.9 11.1 %all-to-all-start.1 = ((bf16[32,64,2048]{2,1,0:T(8,128)(2,1)}), bf16[32,64,2048]{2,1,0:T(8,128)(2,1)}, u32[]{:S(2)}, u32[]{:S(2)}) async-start(bf16[32,64,2048]{2,1,0:T(8,128)(2,1)} %copy.159), calls=%async_computation.1 | async-start | bytes 16777216 | tf_op jit(solution)/shard_map/all_to_all | solution.py:85
  155.0 5.6 copy.166
  160.6 5.6 copy.164
  166.3 88.5 %all-to-all-done.1 = bf16[32,64,2048]{2,1,0:T(8,128)(2,1)} async-done(((bf16[32,64,2048]{2,1,0:T(8,128)(2,1)}), bf16[32,64,2048]{2,1,0:T(8,128)(2,1)}, u32[]{:S(2)}, u32[]{:S(2)}) %all-to-all-start.1) | async-done | bytes 8388640 | tf_op jit(solution)/shard_map/all_to_all | solution.py:85
  254.8 92.6 %while.29 = (s32[]{:T(128)}, f32[4,8,16,64]{3,2,1,0:T(8,128)S(1)}, f32[4,8,16,64]{3,2,1,0:T(8,128)S(1)}, f32[4,8,16,64]{3,2,1,0:T(8,128)S(1)}, bf16[4,8,64,2048]...) while((s32[]{:T(128)}, f32[4,8,16,64]{3,2,1,0:T(8,128)S(1)}, ...), condition=%wide.region_7.8_spmd, body=%wide.region_3.7_spmd.sunk | while | flops 600809472 | bytes 84447416 | solution.py:98
  268.9 6.7 multiply_reduce_fusion.7
  292.0 6.7 multiply_reduce_fusion.7
  315.1 6.7 multiply_reduce_fusion.7
  338.2 6.7 multiply_reduce_fusion.7
  348.3 10.0 %all-to-all-start.3 = ((f32[32,1,1024]{2,1,0:T(1,128)}), f32[32,1,1024]{2,1,0:T(1,128)S(1)}, u32[]{:S(2)}, u32[]{:S(2)}) async-start(f32[32,1,1024]{2,1,0:T(1,128)} %reshape.254), calls=%async_computation.3 | async-start | bytes 262144 | tf_op jit(solution)/shard_map/all_to_all | solution.py:105
  359.1 6.9 all-to-all-done.3
  370.8 6.9 all-to-all-done.6
  398.1 6.9 all-to-all-done.7
  410.1 6.6 all-to-all-done.5
  417.8 349.3 %while.30 = (s32[]{:T(128)}, f32[6,128,2048]{2,0,1:T(8,128)}, f32[6,128,2048]{2,0,1:T(8,128)}, bf16[4,8,64,2048]{3,2,1,0:T(8,128)(2,1)}, bf16[4,8,6]{2,1,0:T(8,1...) while((s32[]{:T(128)}, f32[6,128,2048]{2,0,1:T(8,128)}, ...), condition=%wide.region_13.16_spmd.clone, body=%wide.region_12.15_spmd.clone.sunk | while | flops 1715470336 | bytes 242458960 | solution.py:159
  431.7 6.7 multiply_convert_fusion.2
  450.0 8.5 fusion.112
  458.6 9.5 %copy.253 = f32[8,128,2048]{2,0,1:T(8,128)} copy(f32[8,128,2048]{1,2,0:T(8,128)} %bitcast.179) | data formatting | bytes 16777216 | tf_op jit(solution)/shard_map/while/body/eval_jaxpr/reshape | solution.py:140
  468.0 9.5 %select_add_fusion.5 = f32[6,128,2048]{2,0,1:T(8,128)} fusion(f32[6,128,2048]{2,0,1:T(8,128)} %get-tuple-element.498, f32[8,128,2048]{2,0,1:T(8,128)} %copy.253, pred[]{:T(512)S(6)} %compare.5, bf16[4,8,6]{2,1,0:T(8,128)(2,1)S(1)} %get-tuple-element.513, s32[]{:T(128)S(6)} %copy.275), kind=kOutput, calls=%fused_computation.26.clone.1 | convolution fusion | flops 154140672 | bytes 20973572 | tf_op jit(solution)/shard_map/while/body/eval_jaxpr/sr,stc->rtc/dot_general | solution.py:153
  482.1 9.5 %copy.252 = f32[8,128,2048]{2,0,1:T(8,128)} copy(f32[8,128,2048]{1,2,0:T(8,128)} %bitcast.180) | data formatting | bytes 16777216 | tf_op jit(solution)/shard_map/while/body/eval_jaxpr/reshape | solution.py:143
  491.6 9.5 %select_add_fusion.4 = f32[6,128,2048]{2,0,1:T(8,128)} fusion(f32[6,128,2048]{2,0,1:T(8,128)} %get-tuple-element.497, f32[8,128,2048]{2,0,1:T(8,128)} %copy.252, pred[]{:T(512)S(6)} %compare.5, bf16[4,8,6]{2,1,0:T(8,128)(2,1)S(1)} %get-tuple-element.513, s32[]{:T(128)S(6)} %copy.275), kind=kOutput, calls=%fused_computation.27.clone.1 | convolution fusion | flops 154140672 | bytes 20973572 | tf_op jit(solution)/shard_map/while/body/eval_jaxpr/sr,stc->rtc/dot_general | solution.py:150
  516.4 6.7 multiply_convert_fusion.2
  534.8 8.5 fusion.112
  543.3 9.5 %copy.253 = f32[8,128,2048]{2,0,1:T(8,128)} copy(f32[8,128,2048]{1,2,0:T(8,128)} %bitcast.179) | data formatting | bytes 16777216 | tf_op jit(solution)/shard_map/while/body/eval_jaxpr/reshape | solution.py:140
  552.8 11.2 %select_add_fusion.5 = f32[6,128,2048]{2,0,1:T(8,128)} fusion(f32[6,128,2048]{2,0,1:T(8,128)} %get-tuple-element.498, f32[8,128,2048]{2,0,1:T(8,128)} %copy.253, pred[]{:T(512)S(6)} %compare.5, bf16[4,8,6]{2,1,0:T(8,128)(2,1)S(1)} %get-tuple-element.513, s32[]{:T(128)S(6)} %copy.275), kind=kOutput, calls=%fused_computation.26.clone.1 | convolution fusion | flops 154140672 | bytes 20973572 | tf_op jit(solution)/shard_map/while/body/eval_jaxpr/sr,stc->rtc/dot_general | solution.py:153
  568.5 9.5 %copy.252 = f32[8,128,2048]{2,0,1:T(8,128)} copy(f32[8,128,2048]{1,2,0:T(8,128)} %bitcast.180) | data formatting | bytes 16777216 | tf_op jit(solution)/shard_map/while/body/eval_jaxpr/reshape | solution.py:143
  578.0 11.2 %select_add_fusion.4 = f32[6,128,2048]{2,0,1:T(8,128)} fusion(f32[6,128,2048]{2,0,1:T(8,128)} %get-tuple-element.497, f32[8,128,2048]{2,0,1:T(8,128)} %copy.252, pred[]{:T(512)S(6)} %compare.5, bf16[4,8,6]{2,1,0:T(8,128)(2,1)S(1)} %get-tuple-element.513, s32[]{:T(128)S(6)} %copy.275), kind=kOutput, calls=%fused_computation.27.clone.1 | convolution fusion | flops 154140672 | bytes 20973572 | tf_op jit(solution)/shard_map/while/body/eval_jaxpr/sr,stc->rtc/dot_general | solution.py:150
  604.5 6.7 multiply_convert_fusion.2
  622.9 8.5 fusion.112
  631.4 9.5 %copy.253 = f32[8,128,2048]{2,0,1:T(8,128)} copy(f32[8,128,2048]{1,2,0:T(8,128)} %bitcast.179) | data formatting | bytes 16777216 | tf_op jit(solution)/shard_map/while/body/eval_jaxpr/reshape | solution.py:140
  640.9 11.2 %select_add_fusion.5 = f32[6,128,2048]{2,0,1:T(8,128)} fusion(f32[6,128,2048]{2,0,1:T(8,128)} %get-tuple-element.498, f32[8,128,2048]{2,0,1:T(8,128)} %copy.253, pred[]{:T(512)S(6)} %compare.5, bf16[4,8,6]{2,1,0:T(8,128)(2,1)S(1)} %get-tuple-element.513, s32[]{:T(128)S(6)} %copy.275), kind=kOutput, calls=%fused_computation.26.clone.1 | convolution fusion | flops 154140672 | bytes 20973572 | tf_op jit(solution)/shard_map/while/body/eval_jaxpr/sr,stc->rtc/dot_general | solution.py:153
  656.6 9.5 %copy.252 = f32[8,128,2048]{2,0,1:T(8,128)} copy(f32[8,128,2048]{1,2,0:T(8,128)} %bitcast.180) | data formatting | bytes 16777216 | tf_op jit(solution)/shard_map/while/body/eval_jaxpr/reshape | solution.py:143
  666.1 11.2 %select_add_fusion.4 = f32[6,128,2048]{2,0,1:T(8,128)} fusion(f32[6,128,2048]{2,0,1:T(8,128)} %get-tuple-element.497, f32[8,128,2048]{2,0,1:T(8,128)} %copy.252, pred[]{:T(512)S(6)} %compare.5, bf16[4,8,6]{2,1,0:T(8,128)(2,1)S(1)} %get-tuple-element.513, s32[]{:T(128)S(6)} %copy.275), kind=kOutput, calls=%fused_computation.27.clone.1 | convolution fusion | flops 154140672 | bytes 20973572 | tf_op jit(solution)/shard_map/while/body/eval_jaxpr/sr,stc->rtc/dot_general | solution.py:150
  692.6 6.7 multiply_convert_fusion.2
  710.9 8.5 fusion.112
  719.5 9.5 %copy.253 = f32[8,128,2048]{2,0,1:T(8,128)} copy(f32[8,128,2048]{1,2,0:T(8,128)} %bitcast.179) | data formatting | bytes 16777216 | tf_op jit(solution)/shard_map/while/body/eval_jaxpr/reshape | solution.py:140
  728.9 11.2 %select_add_fusion.5 = f32[6,128,2048]{2,0,1:T(8,128)} fusion(f32[6,128,2048]{2,0,1:T(8,128)} %get-tuple-element.498, f32[8,128,2048]{2,0,1:T(8,128)} %copy.253, pred[]{:T(512)S(6)} %compare.5, bf16[4,8,6]{2,1,0:T(8,128)(2,1)S(1)} %get-tuple-element.513, s32[]{:T(128)S(6)} %copy.275), kind=kOutput, calls=%fused_computation.26.clone.1 | convolution fusion | flops 154140672 | bytes 20973572 | tf_op jit(solution)/shard_map/while/body/eval_jaxpr/sr,stc->rtc/dot_general | solution.py:153
  744.7 9.5 %copy.252 = f32[8,128,2048]{2,0,1:T(8,128)} copy(f32[8,128,2048]{1,2,0:T(8,128)} %bitcast.180) | data formatting | bytes 16777216 | tf_op jit(solution)/shard_map/while/body/eval_jaxpr/reshape | solution.py:143
  754.2 11.2 %select_add_fusion.4 = f32[6,128,2048]{2,0,1:T(8,128)} fusion(f32[6,128,2048]{2,0,1:T(8,128)} %get-tuple-element.497, f32[8,128,2048]{2,0,1:T(8,128)} %copy.252, pred[]{:T(512)S(6)} %compare.5, bf16[4,8,6]{2,1,0:T(8,128)(2,1)S(1)} %get-tuple-element.513, s32[]{:T(128)S(6)} %copy.275), kind=kOutput, calls=%fused_computation.27.clone.1 | convolution fusion | flops 154140672 | bytes 20973572 | tf_op jit(solution)/shard_map/while/body/eval_jaxpr/sr,stc->rtc/dot_general | solution.py:150
  767.1 9.7 %copy.169 = f32[6,128,2048]{2,1,0:T(8,128)} copy(f32[6,128,2048]{2,0,1:T(8,128)} %get-tuple-element.117) | data formatting | bytes 12582912 | tf_op jit(solution)/shard_map/while | solution.py:159
  776.9 9.6 %copy.170 = f32[6,128,2048]{2,1,0:T(8,128)} copy(f32[6,128,2048]{2,0,1:T(8,128)} %get-tuple-element.118) | data formatting | bytes 12582912 | tf_op jit(solution)/shard_map/while | solution.py:159
  791.7 99.7 %all-to-all-done.8 = bf16[32,64,2048]{2,1,0:T(8,128)(2,1)} async-done(((bf16[32,64,2048]{2,1,0:T(8,128)(2,1)}), bf16[32,64,2048]{2,1,0:T(8,128)(2,1)}, u32[]{:S(2)}, u32[]{:S(2)}) %all-to-all-start.8) | async-done | bytes 8388640 | tf_op jit(solution)/shard_map/all_to_all | solution.py:170
  891.3 6.3 gather_fusion
  (241 shorter events, 251.6 us)
Async XLA Ops:
  7.2 13.4 %copy-start = (bf16[8,64,2048]{2,1,0:T(8,128)(2,1)S(1)}, bf16[8,64,2048]{2,1,0:T(8,128)(2,1)}, u32[]{:S(2)}) copy-start(bf16[8,64,2048]{2,1,0:T(8,128)(2,1)} %param.15) | copy-start | bytes 6291460
  8.1 17.2 %copy-start.11 = (s32[8,2]{1,0:T(8,128)}, s32[8,2]{1,0:T(8,128)S(1)}, u32[]{:S(2)}) copy-start(s32[8,2]{1,0:T(8,128)S(1)} %copy.153) | copy-start | bytes 196
  9.3 16.0 %copy-start.13 = (s32[16]{0:T(128)}, s32[16]{0:T(128)S(1)}, u32[]{:S(2)}) copy-start(s32[16]{0:T(128)S(1)} %select_reduce_fusion.1) | copy-start | bytes 196
  10.3 26.2 %all-to-all-start = ((bf16[32,1,6]{2,1,0:T(2,128)(2,1)}), bf16[32,1,6]{2,1,0:T(2,128)(2,1)S(1)}, u32[]{:S(2)}, u32[]{:S(2)}) async-start(bf16[32,1,6]{2,1,0:T(2,128)(2,1)} %copy.155), calls=%async_computation | async-start | bytes 32768 | tf_op jit(solution)/shard_map/all_to_all | solution.py:87
  36.5 8.0 copy-start.10
  36.5 107.4 %all-to-all-start.2 = ((bf16[32,64,2048]{2,1,0:T(8,128)(2,1)}), bf16[32,64,2048]{2,1,0:T(8,128)(2,1)}, u32[]{:S(2)}, u32[]{:S(2)}) async-start(bf16[32,64,2048]{2,1,0:T(8,128)(2,1)} %copy.161), calls=%async_computation.2 | async-start | bytes 16777216 | tf_op jit(solution)/shard_map/all_to_all | solution.py:86
  143.9 110.9 %all-to-all-start.1 = ((bf16[32,64,2048]{2,1,0:T(8,128)(2,1)}), bf16[32,64,2048]{2,1,0:T(8,128)(2,1)}, u32[]{:S(2)}, u32[]{:S(2)}) async-start(bf16[32,64,2048]{2,1,0:T(8,128)(2,1)} %copy.159), calls=%async_computation.1 | async-start | bytes 16777216 | tf_op jit(solution)/shard_map/all_to_all | solution.py:85
  257.5 2.8 copy-start.4
  260.3 2.2 copy-start.3
  280.6 2.8 copy-start.4
  303.7 2.8 copy-start.4
  326.8 2.8 copy-start.4
  348.3 17.8 %all-to-all-start.3 = ((f32[32,1,1024]{2,1,0:T(1,128)}), f32[32,1,1024]{2,1,0:T(1,128)S(1)}, u32[]{:S(2)}, u32[]{:S(2)}) async-start(f32[32,1,1024]{2,1,0:T(1,128)} %reshape.254), calls=%async_computation.3 | async-start | bytes 262144 | tf_op jit(solution)/shard_map/all_to_all | solution.py:105
  366.0 11.7 %all-to-all-start.6 = ((f32[32,1,1024]{2,1,0:T(1,128)}), f32[32,1,1024]{2,1,0:T(1,128)S(1)}, u32[]{:S(2)}, u32[]{:S(2)}) async-start(f32[32,1,1024]{2,1,0:T(1,128)} %reshape.256), calls=%async_computation.6 | async-start | bytes 262144 | tf_op jit(solution)/shard_map/all_to_all | solution.py:107
  377.7 11.7 %all-to-all-start.4 = ((f32[32,1,1024]{2,1,0:T(1,128)}), f32[32,1,1024]{2,1,0:T(1,128)S(1)}, u32[]{:S(2)}, u32[]{:S(2)}) async-start(f32[32,1,1024]{2,1,0:T(1,128)} %reshape.258), calls=%async_computation.4 | async-start | bytes 262144 | tf_op jit(solution)/shard_map/all_to_all | solution.py:106
  393.4 11.7 %all-to-all-start.7 = ((f32[32,1,1024]{2,1,0:T(1,128)}), f32[32,1,1024]{2,1,0:T(1,128)S(1)}, u32[]{:S(2)}, u32[]{:S(2)}) async-start(f32[32,1,1024]{2,1,0:T(1,128)} %reshape.262), calls=%async_computation.7 | async-start | bytes 262144 | tf_op jit(solution)/shard_map/all_to_all | solution.py:122
  405.1 11.7 %all-to-all-start.5 = ((f32[32,1,1024]{2,1,0:T(1,128)}), f32[32,1,1024]{2,1,0:T(1,128)S(1)}, u32[]{:S(2)}, u32[]{:S(2)}) async-start(f32[32,1,1024]{2,1,0:T(1,128)} %reshape.260), calls=%async_computation.5 | async-start | bytes 262144 | tf_op jit(solution)/shard_map/all_to_all | solution.py:121
  409.0 493.5 %reduce-scatter.3.cloned.1.call-start = ((), (), s32[]{:S(2)}) async-start(), calls=%async_computation.11 | async-start | bytes 7864320 | tf_op jit(solution)/shard_map/reduce_scatter | solution.py:176
  418.0 3.6 copy-start.5
  426.7 5.0 copy-start.8
  431.7 6.7 copy-start.2
  438.4 4.7 copy-start.6
  468.0 9.5 %copy-start.7 = (bf16[8,16,64,128]{3,2,1,0:T(8,128)(2,1)S(1)}, bf16[8,16,64,128]{3,2,1,0:T(8,128)(2,1)}, u32[]{:S(2)}) copy-start(bf16[8,16,64,128]{3,2,1,0:T(8,128)(2,1)} %copy-done.6) | copy-start | bytes 6291460 | tf_op jit(solution)/shard_map/while
  491.6 9.6 %copy-start.9 = (bf16[1,8,64,2048]{3,2,1,0:T(8,128)(2,1)S(1)}, bf16[1,8,64,2048]{3,2,1,0:T(8,128)(2,1)}, u32[]{:S(2)}) copy-start(bf16[1,8,64,2048]{3,2,1,0:T(8,128)(2,1)} %broadcast_in_dim.106) | copy-start | bytes 6291460 | tf_op jit(solution)/shard_map/while
  502.7 3.6 copy-start.5
  511.4 5.0 copy-start.8
  516.4 6.7 copy-start.2
  523.2 4.7 copy-start.6
  552.8 11.2 %copy-start.7 = (bf16[8,16,64,128]{3,2,1,0:T(8,128)(2,1)S(1)}, bf16[8,16,64,128]{3,2,1,0:T(8,128)(2,1)}, u32[]{:S(2)}) copy-start(bf16[8,16,64,128]{3,2,1,0:T(8,128)(2,1)} %copy-done.6) | copy-start | bytes 6291460 | tf_op jit(solution)/shard_map/while
  578.0 11.2 %copy-start.9 = (bf16[1,8,64,2048]{3,2,1,0:T(8,128)(2,1)S(1)}, bf16[1,8,64,2048]{3,2,1,0:T(8,128)(2,1)}, u32[]{:S(2)}) copy-start(bf16[1,8,64,2048]{3,2,1,0:T(8,128)(2,1)} %broadcast_in_dim.106) | copy-start | bytes 6291460 | tf_op jit(solution)/shard_map/while
  590.8 3.6 copy-start.5
  599.5 5.0 copy-start.8
  604.5 6.7 copy-start.2
  611.3 4.7 copy-start.6
  640.9 11.2 %copy-start.7 = (bf16[8,16,64,128]{3,2,1,0:T(8,128)(2,1)S(1)}, bf16[8,16,64,128]{3,2,1,0:T(8,128)(2,1)}, u32[]{:S(2)}) copy-start(bf16[8,16,64,128]{3,2,1,0:T(8,128)(2,1)} %copy-done.6) | copy-start | bytes 6291460 | tf_op jit(solution)/shard_map/while
  666.1 11.2 %copy-start.9 = (bf16[1,8,64,2048]{3,2,1,0:T(8,128)(2,1)S(1)}, bf16[1,8,64,2048]{3,2,1,0:T(8,128)(2,1)}, u32[]{:S(2)}) copy-start(bf16[1,8,64,2048]{3,2,1,0:T(8,128)(2,1)} %broadcast_in_dim.106) | copy-start | bytes 6291460 | tf_op jit(solution)/shard_map/while
  678.9 3.6 copy-start.5
  687.6 5.0 copy-start.8
  692.6 6.7 copy-start.2
  699.3 4.7 copy-start.6
  728.9 11.2 %copy-start.7 = (bf16[8,16,64,128]{3,2,1,0:T(8,128)(2,1)S(1)}, bf16[8,16,64,128]{3,2,1,0:T(8,128)(2,1)}, u32[]{:S(2)}) copy-start(bf16[8,16,64,128]{3,2,1,0:T(8,128)(2,1)} %copy-done.6) | copy-start | bytes 6291460 | tf_op jit(solution)/shard_map/while
  754.1 11.2 %copy-start.9 = (bf16[1,8,64,2048]{3,2,1,0:T(8,128)(2,1)S(1)}, bf16[1,8,64,2048]{3,2,1,0:T(8,128)(2,1)}, u32[]{:S(2)}) copy-start(bf16[1,8,64,2048]{3,2,1,0:T(8,128)(2,1)} %broadcast_in_dim.106) | copy-start | bytes 6291460 | tf_op jit(solution)/shard_map/while
  776.9 128.0 %reduce-scatter.5.cloned.1.call-start = ((), (), s32[]{:S(2)}) async-start(), calls=%async_computation.12 | async-start | bytes 7864320 | tf_op jit(solution)/shard_map/reduce_scatter | solution.py:177
  786.5 5.0 copy-start.12
  786.6 5.1 copy-start.14
  786.6 104.7 %all-to-all-start.8 = ((bf16[32,64,2048]{2,1,0:T(8,128)(2,1)}), bf16[32,64,2048]{2,1,0:T(8,128)(2,1)}, u32[]{:S(2)}, u32[]{:S(2)}) async-start(bf16[32,64,2048]{2,1,0:T(8,128)(2,1)} %bitcast.192), calls=%async_computation.8 | async-start | bytes 16777216 | tf_op jit(solution)/shard_map/all_to_all | solution.py:170
  791.6 105.9 %copy-start.15 = (pred[8,2]{1,0:T(8,128)(4,1)S(1)}, pred[8,2]{1,0:T(8,128)(4,1)}, u32[]{:S(2)}) copy-start(pred[8,2]{1,0:T(8,128)(4,1)} %get-tuple-element.297) | copy-start | bytes 52
  897.6 9.8 %copy-start.1 = (bf16[8,64,2048]{2,1,0:T(8,128)(2,1)S(1)}, bf16[8,64,2048]{2,1,0:T(8,128)(2,1)}, u32[]{:S(2)}) copy-start(bf16[8,64,2048]{2,1,0:T(8,128)(2,1)} %param.15) | copy-start | bytes 6291460
  (3 other events, 6.6 us)
Sparse Core Ops, SparseCore 0:
  777.0 61.6 reduce-scatter.2
  841.1 63.6 reduce-scatter.4
where the time goes:
time: 928 us; the launch traced here: 915 us
  waiting for transfers between devices  303 us (33%)
  matrix products  290 us (31%)
  local copies, waits for them, and re-layouts  220 us (24%)
  starting transfers between devices  59.3 us (6%)
  other arithmetic  25.5 us (3%)
  between operations  14.8 us (2%)
    all_to_all x1, waiting for transfers between devices, on_device(): lax.all_to_all(slots_of(query_back), 'retr', split_axis=0, concat_axis=0,...  99.7 us
    all_to_all x1, waiting for transfers between devices, on_device(): lax.all_to_all(send_query, 'retr', split_axis=0, concat_axis=0, tiled=True)  88.5 us
    all_to_all x1, waiting for transfers between devices, on_device(): lax.all_to_all(send_grad, 'retr', split_axis=0, concat_axis=0, tiled=True)  83.5 us
    dot_general x8, matrix products, dprob_for(): jnp.einsum('sqhd,skhd->shqk', head_split(grad_pass, head_count), head_spl...  53.8 us
    dot_general x4, matrix products, gradients(): jnp.einsum('sr,stc->rtc', weights, key_terms, precision=lax.Precision.HIG...  43.2 us
    dot_general x4, matrix products, gradients(): jnp.einsum('sr,stc->rtc', weights, value_terms, precision=lax.Precision.H...  43.1 us
    dot_general x8, matrix products, scores_for(): jnp.einsum('sqhd,skhd->shqk', head_split(query_pass, head_count), head_sp...  40.6 us
    reshape x4, local copies, waits for them, and re-layouts, gradients(): key_terms = jnp.einsum('shqk,sqhd->skhd', dscore, query_heads, preferred_...  37.9 us
  transfers between devices with their start and end apart: 11, of which 8 were waited for; matrix products, arithmetic and copies ran while one was open for 8% of the time, Pallas kernels for 0%

commit v1 on v0

v1 whole, which is shorter than its diff:
```python
import functools

import jax
import jax.numpy as jnp
import numpy as np
from jax import lax
from jax.experimental import pallas as pl
from jax.experimental.pallas import tpu as pltpu
from jax.sharding import Mesh
from jax.sharding import PartitionSpec as P

HD = 128
MiB = 1024 * 1024
ANY = pl.BlockSpec(memory_space=pl.ANY)
VMEM = pl.BlockSpec(memory_space=pltpu.VMEM)
SMEM = pl.BlockSpec(memory_space=pltpu.SMEM)


def place():
    return tuple(lax.axis_index(name) for name in ("y", "z", "x", "c"))


def remote(src, dst, send, recv, where):
    return pltpu.make_async_remote_copy(
        src_ref=src,
        dst_ref=dst,
        send_sem=send,
        recv_sem=recv,
        device_id=where,
        device_id_type=pl.DeviceIdType.MESH,
    )


def greet(nz, nx):
    y, z, x, c = place()
    barrier = pltpu.get_barrier_semaphore()

    def hello(where):
        pl.semaphore_signal(barrier, inc=1, device_id=where, device_id_type=pl.DeviceIdType.MESH)

    @pl.loop(1, nz * nx)
    def _(d):
        hello((y, lax.rem(z + d // nx, nz), lax.rem(x + lax.rem(d, nx), nx), c))

    hello((lax.rem(y + 1, 4), z, x, c))
    hello((lax.rem(y + 3, 4), z, x, c))
    hello((y, z, x, 1 - c))
    pl.semaphore_wait(barrier, nz * nx - 1 + 3)


def bring_kernel(
    nz, nx,
    q_ref, g_ref, k_ref, v_ref, i_ref,
    qh, gh, ka, va, ih,
    s_in, r_in, s_y, r_y, s_c, r_c, own,
):
    y, z, x, c = place()
    chips = nz * nx
    rows = k_ref.shape[0]
    part = chips * rows
    quarter = k_ref.shape[1] // 4
    me = z * nx + x
    up, down, far = lax.rem(y + 1, 4), lax.rem(y + 3, 4), lax.rem(y + 2, 4)
    greet(nz, nx)

    def columns(head):
        return pl.ds(pl.multiple_of(head * HD, HD), HD)

    def token_part(ref, head):
        return ref.at[:, pl.ds(pl.multiple_of(y * quarter, quarter), quarter), columns(head)]

    def landing(ref):
        return ref.at[y, pl.ds(c * part + me * rows, rows)]

    def to_chip(d):
        pz, px = lax.rem(z + d // nx, nz), lax.rem(x + lax.rem(d, nx), nx)
        head = pz * nx + px
        where = (y, pz, px, c)
        return (
            remote(token_part(k_ref, head), landing(ka), s_in.at[0, d], r_in.at[0, d], where),
            remote(token_part(v_ref, head), landing(va), s_in.at[1, d], r_in.at[1, d], where),
            remote(q_ref.at[:, :, columns(head)], qh.at[me], s_in.at[2, d], r_in.at[2, d], where),
            remote(g_ref.at[:, :, columns(head)], gh.at[me], s_in.at[3, d], r_in.at[3, d], where),
            remote(i_ref, ih.at[me], s_in.at[4, d], r_in.at[4, d], where),
        )

    mine = (
        pltpu.make_async_copy(token_part(k_ref, me), landing(ka), own.at[0]),
        pltpu.make_async_copy(token_part(v_ref, me), landing(va), own.at[1]),
        pltpu.make_async_copy(q_ref.at[:, :, columns(me)], qh.at[me], own.at[2]),
        pltpu.make_async_copy(g_ref.at[:, :, columns(me)], gh.at[me], own.at[3]),
        pltpu.make_async_copy(i_ref, ih.at[me], own.at[4]),
    )

    @pl.loop(1, chips)
    def _(d):
        copies = to_chip(d)
        copies[0].start()
        copies[1].start()

    for copy in mine:
        copy.start()

    def chunk(ref, at, core):
        return ref.at[at, pl.ds(core * part, part)]

    def along_y(ref, t, at, slot, where):
        return remote(
            chunk(ref, at, c), chunk(ref, at, c), s_y.at[t, slot], r_y.at[t, slot], (where, z, x, c)
        )

    def across(ref, t, at, slot):
        return remote(
            chunk(ref, at, c), chunk(ref, at, c), s_c.at[t, slot], r_c.at[t, slot], (y, z, x, 1 - c)
        )

    pair = (ka, va)
    for t in (0, 1):

        @pl.loop(1, chips)
        def _(d):
            to_chip(d)[t].wait_recv()

        mine[t].wait()
        along_y(pair[t], t, y, 0, up).start()
        along_y(pair[t], t, y, 1, down).start()
        across(pair[t], t, y, 0).start()

    @pl.loop(1, chips)
    def _(d):
        for copy in to_chip(d)[2:]:
            copy.start()

    for t in (0, 1):
        along_y(pair[t], t, down, 0, up).wait_recv()
        if t == 0:
            along_y(pair[t], t, down, 2, up).start()
        across(pair[t], t, down, 1).start()
        along_y(pair[t], t, up, 1, down).wait_recv()
        if t == 1:
            along_y(pair[t], t, up, 2, down).start()
        across(pair[t], t, up, 2).start()
    for t in (0, 1):
        along_y(pair[t], t, far, 2, up).wait_recv()
        across(pair[t], t, far, 3).start()

    @pl.loop(1, chips)
    def _(d):
        copies = to_chip(d)
        for copy in copies[2:]:
            copy.wait_recv()
        for copy in copies:
            copy.wait_send()

    for copy in mine[2:]:
        copy.wait()
    for t in (0, 1):
        for slot in range(3):
            along_y(pair[t], t, y, slot, up).wait_send()
        for slot in range(4):
            across(pair[t], t, y, slot).wait()


def bring(nz, nx, query, grad_out, keys, values, entry):
    chips = nz * nx
    rows, tokens, _ = keys.shape
    spans, span_len, _ = query.shape
    bf16 = jnp.bfloat16
    held = jax.ShapeDtypeStruct((4, 2 * chips * rows, tokens // 4, HD), bf16)
    heads = jax.ShapeDtypeStruct((chips, spans, span_len, HD), bf16)
    dma = pltpu.SemaphoreType.DMA
    return pl.pallas_call(
        functools.partial(bring_kernel, nz, nx),
        name="bring",
        out_shape=(heads, heads, held, held, jax.ShapeDtypeStruct((chips,) + entry.shape, jnp.int32)),
        in_specs=[ANY] * 5,
        out_specs=(ANY,) * 5,
        scratch_shapes=[
            dma((5, chips)), dma((5, chips)), dma((2, 3)), dma((2, 3)), dma((2, 4)), dma((2, 4)), dma((5,)),
        ],
        compiler_params=pltpu.CompilerParams(collective_id=0, has_side_effects=True),
    )(query, grad_out, keys, values, entry)


def attend_kernel(
    unroll, i_ref, q_ref, g_ref, k_hbm, v_hbm, dq_ref, dk_hbm, dv_hbm, ka, va, dk, dv, sems
):
    fill = (
        pltpu.make_async_copy(k_hbm, ka, sems.at[0]),
        pltpu.make_async_copy(v_hbm, va, sems.at[1]),
    )
    for copy in fill:
        copy.start()
    quarters, rows, tok, _ = ka.shape
    spans = q_ref.shape[0]
    per = i_ref.shape[1]
    scaling = HD ** -0.5
    to_base2 = scaling * float(np.log2(np.e))

    @pl.loop(0, rows)
    def _(r):
        dk[:, r] = jnp.zeros((quarters, tok, HD), jnp.float32)
        dv[:, r] = jnp.zeros((quarters, tok, HD), jnp.float32)

    for copy in fill:
        copy.wait()

    def contract(a, b, da, db):
        return lax.dot_general(
            a, b, (((da,), (db,)), ((), ())), preferred_element_type=jnp.float32
        )

    def row_of(ref, e):
        return ref[:, e].reshape(quarters * tok, HD)

    @pl.loop(0, spans // unroll)
    def _(step):
        results = []
        for u in range(unroll):
            s = step * unroll + u
            e0 = i_ref[s // per, lax.rem(s, per), 0]
            e1 = i_ref[s // per, lax.rem(s, per), 1]
            q, g = q_ref[s], g_ref[s]
            keys = jnp.concatenate([row_of(ka, e0), row_of(ka, e1)], axis=0)
            values = jnp.concatenate([row_of(va, e0), row_of(va, e1)], axis=0)
            scores = contract(q, keys, 1, 1)
            dprob = contract(g, values, 1, 1)
            top = jnp.max(scores, axis=-1, keepdims=True)
            lifted = jnp.exp2((scores - top) * to_base2)
            inverse = 1.0 / jnp.sum(lifted, axis=-1, keepdims=True)
            delta = jnp.sum(lifted * dprob, axis=-1, keepdims=True) * inverse
            chance = lifted * inverse
            chance_low = chance.astype(jnp.bfloat16)
            dscore = ((chance * scaling) * (dprob - delta)).astype(jnp.bfloat16)
            dq_ref[s] = contract(dscore, keys, 1, 0).astype(jnp.bfloat16)
            results.append((e0, e1, contract(dscore, q, 0, 0), contract(chance_low, g, 0, 0)))
        half = quarters * tok
        for e0, e1, key_terms, value_terms in results:
            dk[:, e0] += key_terms[:half].reshape(quarters, tok, HD)
            dk[:, e1] += key_terms[half:].reshape(quarters, tok, HD)
            dv[:, e0] += value_terms[:half].reshape(quarters, tok, HD)
            dv[:, e1] += value_terms[half:].reshape(quarters, tok, HD)

    drain = (
        pltpu.make_async_copy(ka, dk_hbm, sems.at[0]),
        pltpu.make_async_copy(va, dv_hbm, sems.at[1]),
    )
    for low, total, copy in ((ka, dk, drain[0]), (va, dv, drain[1])):

        @pl.loop(0, rows)
        def _(r):
            low[:, r] = total[:, r].astype(jnp.bfloat16)

        copy.start()
    for copy in drain:
        copy.wait()


def attend(entry, qh, gh, ka, va):
    spans = qh.shape[0] * qh.shape[1]
    flat = (spans,) + qh.shape[2:]
    bf16 = jnp.bfloat16
    held = jax.ShapeDtypeStruct(ka.shape, bf16)
    return pl.pallas_call(
        functools.partial(attend_kernel, 2),
        name="attend",
        out_shape=(jax.ShapeDtypeStruct(flat, bf16), held, held),
        in_specs=[SMEM, VMEM, VMEM, ANY, ANY],
        out_specs=(VMEM, ANY, ANY),
        scratch_shapes=[
            pltpu.VMEM(ka.shape, bf16),
            pltpu.VMEM(ka.shape, bf16),
            pltpu.VMEM(ka.shape, jnp.float32),
            pltpu.VMEM(ka.shape, jnp.float32),
            pltpu.SemaphoreType.DMA((2,)),
        ],
        compiler_params=pltpu.CompilerParams(vmem_limit_bytes=56 * MiB),
        cost_estimate=pl.CostEstimate(
            flops=spans * 10 * 64 * 256 * HD, bytes_accessed=32 * MiB, transcendentals=spans * 64 * 256
        ),
    )(entry, qh.reshape(flat), gh.reshape(flat), ka, va)


def give_kernel(
    nz, nx,
    dq_ref, dk_ref, dv_ref,
    gq, gk, gv,
    mine, other, total, passed, arrived,
    s_q, r_q, s_out, r_out, s_c, r_c, s_f, r_f, s_y, r_y, own_q, own_out, own,
):
    y, z, x, c = place()
    chips = nz * nx
    part = mine.shape[2]
    rows = part // chips
    me = z * nx + x
    up, down, far = lax.rem(y + 1, 4), lax.rem(y + 3, 4), lax.rem(y + 2, 4)
    pair = (dk_ref, dv_ref)
    outs = (gk, gv)
    greet(nz, nx)

    at = (far, up, down, y)

    def across(t, slot):
        return remote(
            pair[t].at[at[slot], pl.ds((1 - c) * part, part)], other.at[slot, t],
            s_c.at[slot, t], r_c.at[slot, t], (y, z, x, 1 - c),
        )

    def fetch(t, slot):
        return pltpu.make_async_copy(
            pair[t].at[at[slot], pl.ds(c * part, part)], mine.at[slot, t], own.at[slot, t]
        )

    for slot in range(4):
        for t in (0, 1):
            across(t, slot).start()
            fetch(t, slot).start()

    def columns(head):
        return pl.ds(pl.multiple_of(head * HD, HD), HD)

    def chip(d):
        pz, px = lax.rem(z + d // nx, nz), lax.rem(x + lax.rem(d, nx), nx)
        return pz * nx + px, (y, pz, px, c)

    def query_out(d):
        head, where = chip(d)
        return remote(dq_ref.at[head], gq.at[:, :, columns(me)], s_q.at[d], r_q.at[d], where)

    def key_out(d, t):
        head, where = chip(d)
        return remote(
            total.at[3, t, pl.ds(head * rows, rows)], outs[t].at[:, :, columns(me)],
            s_out.at[t, d], r_out.at[t, d], where,
        )

    query_own = pltpu.make_async_copy(dq_ref.at[me], gq.at[:, :, columns(me)], own_q)
    query_own.start()

    @pl.loop(1, chips)
    def _(d):
        query_out(d).start()

    def f32(a):
        return a.astype(jnp.float32)

    def add(dst, t, slot, *terms):
        @pl.loop(0, part // rows)
        def _(i):
            rs = pl.ds(i * rows, rows)
            sums = f32(terms[0][rs])
            for term in terms[1:]:
                sums = sums + f32(term[rs])
            dst[rs] = sums.astype(jnp.bfloat16)

    def chip_sum(t, slot):
        across(t, slot).wait_recv()
        fetch(t, slot).wait()
        add(total.at[slot, t], t, slot, mine.at[slot, t], other.at[slot, t])

    def far_copy(t):
        return remote(
            total.at[0, t], passed.at[t], s_f.at[t], r_f.at[t], ((up, down)[t], z, x, c)
        )

    def near_copy(t, slot):
        return remote(
            total.at[slot, t], arrived.at[slot - 1, t], s_y.at[slot - 1, t], r_y.at[slot - 1, t],
            ((up, down)[slot - 1], z, x, c),
        )

    for t in (0, 1):
        chip_sum(t, 0)
        far_copy(t).start()
    chip_sum(1, 1)
    near_copy(1, 1).start()
    chip_sum(0, 2)
    near_copy(0, 2).start()
    for t, slot in ((0, 1), (1, 2)):
        across(t, slot).wait_recv()
        fetch(t, slot).wait()
        far_copy(t).wait_recv()
        add(total.at[slot, t], t, slot, mine.at[slot, t], other.at[slot, t], passed.at[t])
        near_copy(t, slot).start()
    for t in (0, 1):
        across(t, 3).wait_recv()
        fetch(t, 3).wait()
    for t in (0, 1):
        near_copy(t, 1).wait_recv()
        near_copy(t, 2).wait_recv()
        add(
            total.at[3, t], t, 3,
            mine.at[3, t], other.at[3, t], arrived.at[0, t], arrived.at[1, t],
        )

        @pl.loop(1, chips)
        def _(d):
            key_out(d, t).start()

        pltpu.make_async_copy(
            total.at[3, t, pl.ds(me * rows, rows)], outs[t].at[:, :, columns(me)], own_out.at[t]
        ).start()

    @pl.loop(1, chips)
    def _(d):
        query_out(d).wait()
        for t in (0, 1):
            key_out(d, t).wait()

    query_own.wait()
    for t in (0, 1):
        pltpu.make_async_copy(
            total.at[3, t, pl.ds(me * rows, rows)], outs[t].at[:, :, columns(me)], own_out.at[t]
        ).wait()
        far_copy(t).wait_send()
        for slot in range(4):
            across(t, slot).wait_send()
        for slot in (1, 2):
            near_copy(t, slot).wait_send()


def give(nz, nx, dq, dk, dv):
    chips = nz * nx
    _, all_rows, tok, _ = dk.shape
    part = all_rows // 2
    _, spans, span_len, _ = dq.shape
    bf16 = jnp.bfloat16
    dma = pltpu.SemaphoreType.DMA
    row_out = jax.ShapeDtypeStruct((part // chips, tok, chips * HD), bf16)
    return pl.pallas_call(
        functools.partial(give_kernel, nz, nx),
        name="give",
        out_shape=(jax.ShapeDtypeStruct((spans, span_len, chips * HD), bf16), row_out, row_out),
        in_specs=[ANY] * 3,
        out_specs=(ANY,) * 3,
        scratch_shapes=[
            pltpu.VMEM((4, 2, part, tok, HD), bf16),
            pltpu.VMEM((4, 2, part, tok, HD), bf16),
            pltpu.VMEM((4, 2, part, tok, HD), bf16),
            pltpu.VMEM((2, part, tok, HD), bf16),
            pltpu.VMEM((2, 2, part, tok, HD), bf16),
            dma((chips,)), dma((chips,)), dma((2, chips)), dma((2, chips)),
            dma((4, 2)), dma((4, 2)), dma((2,)), dma((2,)), dma((2, 2)), dma((2, 2)),
            dma, dma((2,)), dma((4, 2)),
        ],
        compiler_params=pltpu.CompilerParams(
            collective_id=1, has_side_effects=True, vmem_limit_bytes=48 * MiB
        ),
    )(dq, dk, dv)


def on_device(nz, nx, query, grad_out, keys, values, owner_list, row_list):
    chips = nz * nx
    rows = keys.shape[0]
    entry = lax.rem(owner_list, 2) * (chips * rows) + (owner_list // 2) * rows + row_list
    entry = jnp.pad(entry, ((0, 0), (0, HD - entry.shape[1])))
    qh, gh, ka, va, ih = bring(nz, nx, query, grad_out, keys, values, entry)
    dq, dk, dv = attend(ih, qh, gh, ka, va)
    return give(nz, nx, dq.reshape(qh.shape), dk, dv)


def solution(mesh):
    groups, retr = mesh.devices.shape
    nx = 4 if retr == 32 else 2
    nz = retr // (2 * nx)
    fine = Mesh(mesh.devices.reshape(groups, nz, nx, 2), ("y", "z", "x", "c"))
    all_axes = ("y", "z", "x", "c")
    owner = ("z", "x", "c")
    return jax.shard_map(
        functools.partial(on_device, nz, nx),
        mesh=fine,
        in_specs=(
            P(all_axes, None, None),
            P(all_axes, None, None),
            P(owner, None, None),
            P(owner, None, None),
            P(all_axes, None),
            P(all_axes, None),
        ),
        out_specs=(P(all_axes, None, None), P(owner, "y", None), P(owner, "y", None)),
        check_vma=False,
    )
```

time: 928 us -> 268 us (0.29); the launches traced: 915 us -> 268 us
  waiting for transfers between devices: 303 us -> 0 us
  matrix products: 290 us -> 0 us
  Pallas kernels: 0 us -> 260 us
  local copies, waits for them, and re-layouts: 220 us -> 6.77 us
  starting transfers between devices: 59.3 us -> 0 us
  other arithmetic: 25.5 us -> 0.01 us
  between operations: 14.8 us -> 0.67 us
    all_to_all x9 -> x0, waiting for transfers between devices: 303 us -> none  [the longest x1 99.7 us: on_device(): lax.all_to_all(slots_of(query_back), 'retr', split_axis=0, concat_axis=0,...]
    dot_general x55 -> x0, matrix products: 290 us -> none  [the longest x8 53.8 us: dprob_for(): jnp.einsum('sqhd,skhd->shqk', head_split(grad_pass, head_count), head_spl...]
    pallas_call x0 -> x3, Pallas kernels: none -> 260 us  [the longest x1 93.7 us: bring(): pl.pallas_call(functools.partial(bring_kernel, nz, nx), name='bring', out...]
    reshape x10 -> x0, local copies, waits for them, and re-layouts: 75.9 us -> none  [the longest x4 37.9 us: gradients(): key_terms = jnp.einsum('shqk,sqhd->skhd', dscore, query_heads, preferred_...]
    all_to_all x9 -> x0, starting transfers between devices: 59.2 us -> none  [the longest x1 11.1 us: on_device(): lax.all_to_all(send_query, 'retr', split_axis=0, concat_axis=0, tiled=True)]
    while x83 -> x0, local copies, waits for them, and re-layouts: 39.9 us -> none  [the longest x2 19.3 us: on_device(): lax.scan(gradients, (zero_rows, zero_rows), (passes_of(got_query), passes...]
    convert_element_type x6 -> x0, local copies, waits for them, and re-layouts: 33.4 us -> none  [the longest x1 11.2 us: on_device(): send_grad = jnp.einsum('sc,ctd->std', by_span, grad_out, preferred_elemen...]
    dynamic_slice x12 -> x0, local copies, waits for them, and re-layouts: 25.3 us -> none  [on_device(): lax.map(first_pass, (passes_of(got_query), passes_of(got_grad), passes_of...]
  transfers between devices with their start and end apart: 11 -> 0, of which waited for: 8 -> 0; matrix products, arithmetic and copies ran while one was open for 8% -> 0% of each run, Pallas kernels for 0% -> 0%
where the time goes in v1:
time: 268 us
  Pallas kernels  260 us (97%)
  local copies, waits for them, and re-layouts  6.77 us (3%)
    pallas_call x1, Pallas kernels, bring(): pl.pallas_call(functools.partial(bring_kernel, nz, nx), name='bring', out...  93.7 us
    pallas_call x1, Pallas kernels, give(): pl.pallas_call(functools.partial(give_kernel, nz, nx), name='give', out_s...  91.3 us
    pallas_call x1, Pallas kernels, attend(): pl.pallas_call(functools.partial(attend_kernel, 2), name='attend', out_sh...  75.4 us
    unnamed x7, local copies, waits for them, and re-layouts  6.17 us

profile of v1, /device:TPU:1, one launch (start us, length us, event | category | flops | bytes accessed | tf_op | source)
XLA Modules:
  0.0 267.8 jit_solution(1030041256119649601)
XLA Ops:
  0.6 0.8 copy.9
  1.4 0.8 copy.13
  2.2 0.6 pad.4.i_ref
  2.8 93.7 %bring.1 = (bf16[16,8,64,128]{3,2,1,0:T(8,128)(2,1)}, bf16[16,8,64,128]{3,2,1,0:T(8,128)(2,1)}, bf16[4,192,32,128]{3,2,1,0:T(8,128)(2,1)}, bf16[4,192,32,128]{3,2,1,0:T(8,128)(2,1)}, s32[16,8,128]{2,1,0:T(8,128)}) custom-call(bf16[8,64,2048]{2,1,0:T(8,128)(2,1)} %q_ref.1, bf16[8,64,2048]{2,1,0:T(8,128)(2,1)} %g_ref.1, bf16[6,128,2048]{2,1,0:T(8,128)(2,1)} %k_ref.1, ...), custom_call_target="tpu_custom_call" | custom-call | tf_op jit(solution)/shard_map/bring/pallas_call | solution.py:172
  96.4 75.4 %attend.1 = (bf16[128,64,128]{2,1,0:T(8,128)(2,1)}, bf16[4,192,32,128]{3,2,1,0:T(8,128)(2,1)}, bf16[4,192,32,128]{3,2,1,0:T(8,128)(2,1)}) custom-call(s32[16,8,128]{2,1,0:T(8,128)} %get-tuple-element.11.i_ref, bf16[128,64,128]{2,1,0:T(8,128)(2,1)} %bitcast.4, bf16[128,64,128]{2,1,0:T(8,128)(2,1)} %bitcast.5, ...), custom_call_target="tpu_custom_call" | custom-call | flops 2684354560 | bytes 33554432 | tf_op jit(solution)/shard_map/attend/pallas_call | solution.py:264
  171.8 0.0 copy-start
  171.9 1.6 copy-done
  173.4 91.3 %give.1 = (bf16[8,64,2048]{2,1,0:T(8,128)(2,1)S(1)}, bf16[6,32,2048]{2,1,0:T(8,128)(2,1)S(1)}, bf16[6,32,2048]{2,1,0:T(8,128)(2,1)S(1)}) custom-call(bf16[16,8,64,128]{3,2,1,0:T(8,128)(2,1)S(1)} %bitcast.3, bf16[4,192,32,128]{3,2,1,0:T(8,128)(2,1)} %get-tuple-element.17.dk_ref, bf16[4,192,32,128]{3,2,1,0:T(8,128)(2,1)} %get-tuple-element.18.dv_ref), custom_call_target="tpu_custom_call" | custom-call | tf_op jit(solution)/shard_map/give/pallas_call | solution.py:430
  264.7 1.3 copy.17
  266.0 0.9 copy.18
  266.9 0.9 copy.19
  (1 shorter events, 0.0 us)
Async XLA Ops:
  171.8 1.6 copy-start

commit v2 on v1

v2 whole, which is shorter than its diff:
```python
import functools

import jax
import jax.numpy as jnp
import numpy as np
from jax import lax
from jax.experimental import pallas as pl
from jax.experimental.pallas import tpu as pltpu
from jax.sharding import Mesh
from jax.sharding import PartitionSpec as P

HD = 128
MiB = 1024 * 1024
ANY = pl.BlockSpec(memory_space=pl.ANY)
VMEM = pl.BlockSpec(memory_space=pltpu.VMEM)
SMEM = pl.BlockSpec(memory_space=pltpu.SMEM)


def place():
    return tuple(lax.axis_index(name) for name in ("y", "z", "x", "c"))


def remote(src, dst, send, recv, where):
    return pltpu.make_async_remote_copy(
        src_ref=src,
        dst_ref=dst,
        send_sem=send,
        recv_sem=recv,
        device_id=where,
        device_id_type=pl.DeviceIdType.MESH,
    )


def greet(nz, nx):
    y, z, x, c = place()
    barrier = pltpu.get_barrier_semaphore()

    def hello(where):
        pl.semaphore_signal(barrier, inc=1, device_id=where, device_id_type=pl.DeviceIdType.MESH)

    @pl.loop(1, nz * nx)
    def _(d):
        hello((y, lax.rem(z + d // nx, nz), lax.rem(x + lax.rem(d, nx), nx), c))

    hello((lax.rem(y + 1, 4), z, x, c))
    hello((lax.rem(y + 3, 4), z, x, c))
    hello((y, z, x, 1 - c))
    pl.semaphore_wait(barrier, nz * nx - 1 + 3)


def offsets(nz, nx):
    steps = [(dz, dx) for dz in range(nz) for dx in range(nx) if dz or dx]

    def hops(step):
        return min(step[0], nz - step[0]) + min(step[1], nx - step[1])

    return sorted(steps, key=hops)


def bring_kernel(
    nz, nx,
    q_ref, g_ref, k_ref, v_ref, i_ref,
    qh, gh, ka, va, ih,
    s_in, r_in, s_y, r_y, s_c, r_c, own,
):
    y, z, x, c = place()
    chips = nz * nx
    rows = k_ref.shape[0]
    part = chips * rows
    quarter = k_ref.shape[1] // 4
    me = z * nx + x
    up, down, far = lax.rem(y + 1, 4), lax.rem(y + 3, 4), lax.rem(y + 2, 4)
    greet(nz, nx)

    def columns(head):
        return pl.ds(pl.multiple_of(head * HD, HD), HD)

    def token_part(ref, head):
        return ref.at[:, pl.ds(pl.multiple_of(y * quarter, quarter), quarter), columns(head)]

    def landing(ref):
        return ref.at[y, pl.ds(c * part + me * rows, rows)]

    def sides(t, head):
        if t < 2:
            return token_part((k_ref, v_ref)[t], head), landing((ka, va)[t])
        if t < 4:
            return (q_ref, g_ref)[t - 2].at[:, :, columns(head)], (qh, gh)[t - 2].at[me]
        return i_ref, ih.at[me]

    def to_chip(t, d):
        pz, px = lax.rem(z + d // nx, nz), lax.rem(x + lax.rem(d, nx), nx)
        return remote(*sides(t, pz * nx + px), s_in.at[t, d], r_in.at[t, d], (y, pz, px, c))

    def keep(t):
        return pltpu.make_async_copy(*sides(t, me), own.at[t])

    def arrived(t):
        @pl.loop(1, chips)
        def _(d):
            to_chip(t, d).wait_recv()

        keep(t).wait()

    for t in (0, 1, 4, 2, 3):
        for dz, dx in offsets(nz, nx):
            to_chip(t, dz * nx + dx).start()
        keep(t).start()

    def chunk(t, at):
        return (ka, va)[t].at[at, pl.ds(c * part, part)]

    def along_y(t, at, slot, where):
        return remote(
            chunk(t, at), chunk(t, at), s_y.at[t, slot], r_y.at[t, slot], (where, z, x, c)
        )

    def across(t, at, slot):
        return remote(
            chunk(t, at), chunk(t, at), s_c.at[t, slot], r_c.at[t, slot], (y, z, x, 1 - c)
        )

    for t in (0, 1):
        arrived(t)
        along_y(t, y, 0, up).start()
        along_y(t, y, 1, down).start()
        across(t, y, 0).start()

    for t in (0, 1):
        along_y(t, down, 0, up).wait_recv()
        if t == 0:
            along_y(t, down, 2, up).start()
        across(t, down, 1).start()
        along_y(t, up, 1, down).wait_recv()
        if t == 1:
            along_y(t, up, 2, down).start()
        across(t, up, 2).start()
    for t in (0, 1):
        along_y(t, far, 2, up).wait_recv()
        across(t, far, 3).start()

    for t in (2, 3, 4):
        arrived(t)
    for t in range(5):

        @pl.loop(1, chips)
        def _(d):
            to_chip(t, d).wait_send()

    for t in (0, 1):
        for slot in range(3):
            along_y(t, y, slot, up).wait_send()
        for slot in range(4):
            across(t, y, slot).wait()


def bring(nz, nx, query, grad_out, keys, values, entry):
    chips = nz * nx
    rows, tokens, _ = keys.shape
    spans, span_len, _ = query.shape
    bf16 = jnp.bfloat16
    held = jax.ShapeDtypeStruct((4, 2 * chips * rows, tokens // 4, HD), bf16)
    heads = jax.ShapeDtypeStruct((chips, spans, span_len, HD), bf16)
    dma = pltpu.SemaphoreType.DMA
    return pl.pallas_call(
        functools.partial(bring_kernel, nz, nx),
        name="bring",
        out_shape=(heads, heads, held, held, jax.ShapeDtypeStruct((chips,) + entry.shape, jnp.int32)),
        in_specs=[ANY] * 5,
        out_specs=(ANY,) * 5,
        scratch_shapes=[
            dma((5, chips)), dma((5, chips)), dma((2, 3)), dma((2, 3)), dma((2, 4)), dma((2, 4)), dma((5,)),
        ],
        compiler_params=pltpu.CompilerParams(collective_id=0, has_side_effects=True),
    )(query, grad_out, keys, values, entry)


def attend_kernel(
    unroll, i_ref, q_ref, g_ref, k_hbm, v_hbm, dq_ref, dk_hbm, dv_hbm, ka, va, dk, dv, sems
):
    fill = (
        pltpu.make_async_copy(k_hbm, ka, sems.at[0]),
        pltpu.make_async_copy(v_hbm, va, sems.at[1]),
    )
    for copy in fill:
        copy.start()
    quarters, rows, tok, _ = ka.shape
    spans, span_len, _ = q_ref.shape
    tokens = quarters * tok
    per = i_ref.shape[1]
    scaling = HD ** -0.5
    to_base2 = scaling * float(np.log2(np.e))

    @pl.loop(0, rows)
    def _(r):
        dk[:, r] = jnp.zeros((quarters, tok, HD), jnp.float32)
        dv[:, r] = jnp.zeros((quarters, tok, HD), jnp.float32)

    for copy in fill:
        copy.wait()

    def contract(a, b, da, db):
        return lax.dot_general(
            a, b, (((da,), (db,)), ((), ())), preferred_element_type=jnp.float32
        )

    def rows_of(ref, ea, eb):
        return jnp.concatenate(
            [ref[:, ea].reshape(tokens, HD), ref[:, eb].reshape(tokens, HD)], axis=0
        )

    def diagonal(a, b):
        empty = jnp.zeros_like(a)
        return jnp.concatenate(
            [jnp.concatenate([a, empty], axis=1), jnp.concatenate([empty, b], axis=1)], axis=0
        )

    def gradients(sa):
        sb = sa + 1
        entries = [i_ref[s // per, lax.rem(s, per), n] for s in (sa, sb) for n in (0, 1)]
        queries = diagonal(q_ref[sa], q_ref[sb])
        grads = diagonal(g_ref[sa], g_ref[sb])
        keys = jnp.concatenate([rows_of(ka, *entries[:2]), rows_of(ka, *entries[2:])], axis=1)
        values = jnp.concatenate([rows_of(va, *entries[:2]), rows_of(va, *entries[2:])], axis=1)
        scores = contract(keys, queries, 1, 1)
        dprob = contract(values, grads, 1, 1)
        top = jnp.max(scores, axis=0, keepdims=True)
        lifted = jnp.exp2((scores - top) * to_base2)
        inverse = 1.0 / jnp.sum(lifted, axis=0, keepdims=True)
        delta = jnp.sum(lifted * dprob, axis=0, keepdims=True) * inverse
        chance_low = (lifted * inverse).astype(jnp.bfloat16)
        dscore = (lifted * (inverse * scaling) * (dprob - delta)).astype(jnp.bfloat16)
        both = contract(dscore, keys, 0, 0)
        dq_ref[sa] = both[:span_len, :HD].astype(jnp.bfloat16)
        dq_ref[sb] = both[span_len:, HD:].astype(jnp.bfloat16)
        return entries, contract(dscore, queries, 1, 0), contract(chance_low, grads, 1, 0)

    @pl.loop(0, spans // (2 * unroll))
    def _(step):
        results = [gradients(2 * (step * unroll + u)) for u in range(unroll)]
        for entries, key_terms, value_terms in results:
            for at, e in enumerate(entries):
                rs = slice(at % 2 * tokens, (at % 2 + 1) * tokens)
                cs = slice(at // 2 * HD, (at // 2 + 1) * HD)
                dk[:, e] += key_terms[rs, cs].reshape(quarters, tok, HD)
                dv[:, e] += value_terms[rs, cs].reshape(quarters, tok, HD)

    drain = (
        pltpu.make_async_copy(ka, dk_hbm, sems.at[0]),
        pltpu.make_async_copy(va, dv_hbm, sems.at[1]),
    )
    for low, total, copy in ((ka, dk, drain[0]), (va, dv, drain[1])):

        @pl.loop(0, rows)
        def _(r):
            low[:, r] = total[:, r].astype(jnp.bfloat16)

        copy.start()
    for copy in drain:
        copy.wait()


def attend(entry, qh, gh, ka, va):
    spans = qh.shape[0] * qh.shape[1]
    flat = (spans,) + qh.shape[2:]
    bf16 = jnp.bfloat16
    held = jax.ShapeDtypeStruct(ka.shape, bf16)
    return pl.pallas_call(
        functools.partial(attend_kernel, min(4, spans // 2)),
        name="attend",
        out_shape=(jax.ShapeDtypeStruct(flat, bf16), held, held),
        in_specs=[SMEM, VMEM, VMEM, ANY, ANY],
        out_specs=(VMEM, ANY, ANY),
        scratch_shapes=[
            pltpu.VMEM(ka.shape, bf16),
            pltpu.VMEM(ka.shape, bf16),
            pltpu.VMEM(ka.shape, jnp.float32),
            pltpu.VMEM(ka.shape, jnp.float32),
            pltpu.SemaphoreType.DMA((2,)),
        ],
        compiler_params=pltpu.CompilerParams(vmem_limit_bytes=56 * MiB),
        cost_estimate=pl.CostEstimate(
            flops=spans * 10 * 64 * 256 * HD, bytes_accessed=32 * MiB, transcendentals=spans * 64 * 256
        ),
    )(entry, qh.reshape(flat), gh.reshape(flat), ka, va)


def give_kernel(
    nz, nx,
    dq_ref, dk_ref, dv_ref,
    gq, gk, gv,
    mine, other, total, passed, arrived,
    s_q, r_q, s_out, r_out, s_c, r_c, s_f, r_f, s_y, r_y, own_q, own_out, own,
):
    y, z, x, c = place()
    chips = nz * nx
    part = chips * (gk.shape[0])
    rows = part // chips
    band = nx * rows
    me = z * nx + x
    up, down, far = lax.rem(y + 1, 4), lax.rem(y + 3, 4), lax.rem(y + 2, 4)
    pair = (dk_ref, dv_ref)
    outs = (gk, gv)
    greet(nz, nx)

    at = (far, up, down, y)
    bands = sorted(range(nz), key=lambda dz: -min(dz, nz - dz))

    def first_row(dz):
        return lax.rem(z + dz, nz) * band

    def across(t, slot, dz):
        return remote(
            pair[t].at[at[slot], pl.ds((1 - c) * part + first_row(dz), band)],
            other.at[slot, t, dz],
            s_c.at[slot, t, dz], r_c.at[slot, t, dz], (y, z, x, 1 - c),
        )

    def fetch(t, slot, dz):
        return pltpu.make_async_copy(
            pair[t].at[at[slot], pl.ds(c * part + first_row(dz), band)],
            mine.at[slot, t, dz],
            own.at[slot, t, dz],
        )

    for dz in bands:
        for slot in range(4):
            for t in (0, 1):
                across(t, slot, dz).start()
                fetch(t, slot, dz).start()

    def columns(head):
        return pl.ds(pl.multiple_of(head * HD, HD), HD)

    def chip(d):
        pz, px = lax.rem(z + d // nx, nz), lax.rem(x + lax.rem(d, nx), nx)
        return pz * nx + px, (y, pz, px, c)

    def query_out(d):
        head, where = chip(d)
        return remote(dq_ref.at[head], gq.at[:, :, columns(me)], s_q.at[d], r_q.at[d], where)

    def key_out(d, t):
        _, where = chip(d)
        px = lax.rem(x + lax.rem(d, nx), nx)
        return remote(
            total.at[3, t, d // nx, pl.ds(px * rows, rows)], outs[t].at[:, :, columns(me)],
            s_out.at[t, d], r_out.at[t, d], where,
        )

    def key_own(t):
        return pltpu.make_async_copy(
            total.at[3, t, 0, pl.ds(x * rows, rows)], outs[t].at[:, :, columns(me)], own_out.at[t]
        )

    query_own = pltpu.make_async_copy(dq_ref.at[me], gq.at[:, :, columns(me)], own_q)
    query_own.start()
    for dz, dx in offsets(nz, nx):
        query_out(dz * nx + dx).start()

    def f32(a):
        return a.astype(jnp.float32)

    def add(dst, *terms):
        @pl.loop(0, band // rows)
        def _(i):
            rs = pl.ds(i * rows, rows)
            sums = f32(terms[0][rs])
            for term in terms[1:]:
                sums = sums + f32(term[rs])
            dst[rs] = sums.astype(jnp.bfloat16)

    def both_cores(t, slot, dz):
        across(t, slot, dz).wait_recv()
        fetch(t, slot, dz).wait()
        return mine.at[slot, t, dz], other.at[slot, t, dz]

    def far_copy(t, dz):
        return remote(
            total.at[0, t, dz], passed.at[t, dz], s_f.at[t, dz], r_f.at[t, dz],
            ((up, down)[t], z, x, c),
        )

    def near_copy(t, slot, dz):
        return remote(
            total.at[slot, t, dz], arrived.at[slot - 1, t, dz],
            s_y.at[slot - 1, t, dz], r_y.at[slot - 1, t, dz],
            ((up, down)[slot - 1], z, x, c),
        )

    def direct(dz):
        for t in (0, 1):
            add(total.at[0, t, dz], *both_cores(t, 0, dz))
            far_copy(t, dz).start()
        for t, slot in ((1, 1), (0, 2)):
            add(total.at[slot, t, dz], *both_cores(t, slot, dz))
            near_copy(t, slot, dz).start()

    def merged(dz):
        for t, slot in ((0, 1), (1, 2)):
            terms = both_cores(t, slot, dz)
            far_copy(t, dz).wait_recv()
            add(total.at[slot, t, dz], *terms, passed.at[t, dz])
            near_copy(t, slot, dz).start()

    def final(dz):
        for t in (0, 1):
            terms = both_cores(t, 3, dz)
            near_copy(t, 1, dz).wait_recv()
            near_copy(t, 2, dz).wait_recv()
            add(total.at[3, t, dz], *terms, arrived.at[0, t, dz], arrived.at[1, t, dz])
            for dx in range(nx):
                if dz or dx:
                    key_out(dz * nx + dx, t).start()
                else:
                    key_own(t).start()

    for step in range(nz + 2):
        if step < nz:
            direct(bands[step])
        if 1 <= step < nz + 1:
            merged(bands[step - 1])
        if step >= 2:
            final(bands[step - 2])

    @pl.loop(1, chips)
    def _(d):
        query_out(d).wait()
        for t in (0, 1):
            key_out(d, t).wait()

    query_own.wait()
    for t in (0, 1):
        key_own(t).wait()

        @pl.loop(0, nz)
        def _(dz):
            far_copy(t, dz).wait_send()
            for slot in range(4):
                across(t, slot, dz).wait_send()
            for slot in (1, 2):
                near_copy(t, slot, dz).wait_send()


def give(nz, nx, dq, dk, dv):
    chips = nz * nx
    _, all_rows, tok, _ = dk.shape
    part = all_rows // 2
    band = part // nz
    _, spans, span_len, _ = dq.shape
    bf16 = jnp.bfloat16
    dma = pltpu.SemaphoreType.DMA
    row_out = jax.ShapeDtypeStruct((part // chips, tok, chips * HD), bf16)
    return pl.pallas_call(
        functools.partial(give_kernel, nz, nx),
        name="give",
        out_shape=(jax.ShapeDtypeStruct((spans, span_len, chips * HD), bf16), row_out, row_out),
        in_specs=[ANY] * 3,
        out_specs=(ANY,) * 3,
        scratch_shapes=[
            pltpu.VMEM((4, 2, nz, band, tok, HD), bf16),
            pltpu.VMEM((4, 2, nz, band, tok, HD), bf16),
            pltpu.VMEM((4, 2, nz, band, tok, HD), bf16),
            pltpu.VMEM((2, nz, band, tok, HD), bf16),
            pltpu.VMEM((2, 2, nz, band, tok, HD), bf16),
            dma((chips,)), dma((chips,)), dma((2, chips)), dma((2, chips)),
            dma((4, 2, nz)), dma((4, 2, nz)), dma((2, nz)), dma((2, nz)),
            dma((2, 2, nz)), dma((2, 2, nz)), dma, dma((2,)), dma((4, 2, nz)),
        ],
        compiler_params=pltpu.CompilerParams(
            collective_id=1, has_side_effects=True, vmem_limit_bytes=48 * MiB
        ),
    )(dq, dk, dv)


def on_device(nz, nx, query, grad_out, keys, values, owner_list, row_list):
    chips = nz * nx
    rows = keys.shape[0]
    entry = lax.rem(owner_list, 2) * (chips * rows) + (owner_list // 2) * rows + row_list
    entry = jnp.pad(entry, ((0, 0), (0, HD - entry.shape[1])))
    qh, gh, ka, va, ih = bring(nz, nx, query, grad_out, keys, values, entry)
    dq, dk, dv = attend(ih, qh, gh, ka, va)
    return give(nz, nx, dq.reshape(qh.shape), dk, dv)


def solution(mesh):
    groups, retr = mesh.devices.shape
    nx = 4 if retr == 32 else 2
    nz = retr // (2 * nx)
    fine = Mesh(mesh.devices.reshape(groups, nz, nx, 2), ("y", "z", "x", "c"))
    all_axes = ("y", "z", "x", "c")
    owner = ("z", "x", "c")
    return jax.shard_map(
        functools.partial(on_device, nz, nx),
        mesh=fine,
        in_specs=(
            P(all_axes, None, None),
            P(all_axes, None, None),
            P(owner, None, None),
            P(owner, None, None),
            P(all_axes, None),
            P(all_axes, None),
        ),
        out_specs=(P(all_axes, None, None), P(owner, "y", None), P(owner, "y", None)),
        check_vma=False,
    )
```

time: 268 us -> 195 us (0.73)
  Pallas kernels: 260 us -> 188 us
    pallas_call x1, Pallas kernels: 75.4 us -> 40.4 us  [attend(): pl.pallas_call(functools.partial(attend_kernel, min(4, spans // 2)), name...]
    pallas_call x1, Pallas kernels: 91.3 us -> 69.4 us  [give(): pl.pallas_call(functools.partial(give_kernel, nz, nx), name='give', out_s...]
    pallas_call x1, Pallas kernels: 93.7 us -> 77.9 us  [bring(): pl.pallas_call(functools.partial(bring_kernel, nz, nx), name='bring', out...]
where the time goes in v2:
time: 195 us
  Pallas kernels  188 us (96%)
  local copies, waits for them, and re-layouts  6.77 us (3%)
    pallas_call x1, Pallas kernels, bring(): pl.pallas_call(functools.partial(bring_kernel, nz, nx), name='bring', out...  77.9 us
    pallas_call x1, Pallas kernels, give(): pl.pallas_call(functools.partial(give_kernel, nz, nx), name='give', out_s...  69.4 us
    pallas_call x1, Pallas kernels, attend(): pl.pallas_call(functools.partial(attend_kernel, min(4, spans // 2)), name...  40.4 us
    unnamed x7, local copies, waits for them, and re-layouts  6.17 us

profile of v2, /device:TPU:1, one launch (start us, length us, event | category | flops | bytes accessed | tf_op | source)
XLA Modules:
  0.0 195.2 jit_solution(6040714735147506206)
XLA Ops:
  0.6 0.8 copy.9
  1.4 0.8 copy.13
  2.2 0.6 pad.4.i_ref
  2.8 77.9 %bring.1 = (bf16[16,8,64,128]{3,2,1,0:T(8,128)(2,1)}, bf16[16,8,64,128]{3,2,1,0:T(8,128)(2,1)}, bf16[4,192,32,128]{3,2,1,0:T(8,128)(2,1)}, bf16[4,192,32,128]{3,2,1,0:T(8,128)(2,1)}, s32[16,8,128]{2,1,0:T(8,128)}) custom-call(bf16[8,64,2048]{2,1,0:T(8,128)(2,1)} %q_ref.1, bf16[8,64,2048]{2,1,0:T(8,128)(2,1)} %g_ref.1, bf16[6,128,2048]{2,1,0:T(8,128)(2,1)} %k_ref.1, ...), custom_call_target="tpu_custom_call" | custom-call | tf_op jit(solution)/shard_map/bring/pallas_call | solution.py:165
  80.7 40.4 %attend.1 = (bf16[128,64,128]{2,1,0:T(8,128)(2,1)}, bf16[4,192,32,128]{3,2,1,0:T(8,128)(2,1)}, bf16[4,192,32,128]{3,2,1,0:T(8,128)(2,1)}) custom-call(s32[16,8,128]{2,1,0:T(8,128)} %get-tuple-element.11.i_ref, bf16[128,64,128]{2,1,0:T(8,128)(2,1)} %bitcast.4, bf16[128,64,128]{2,1,0:T(8,128)(2,1)} %bitcast.5, ...), custom_call_target="tpu_custom_call" | custom-call | flops 2684354560 | bytes 33554432 | tf_op jit(solution)/shard_map/attend/pallas_call | solution.py:268
  121.1 0.0 copy-start
  121.1 1.6 copy-done
  122.7 69.4 %give.1 = (bf16[8,64,2048]{2,1,0:T(8,128)(2,1)S(1)}, bf16[6,32,2048]{2,1,0:T(8,128)(2,1)S(1)}, bf16[6,32,2048]{2,1,0:T(8,128)(2,1)S(1)}) custom-call(bf16[16,8,64,128]{3,2,1,0:T(8,128)(2,1)S(1)} %bitcast.3, bf16[4,192,32,128]{3,2,1,0:T(8,128)(2,1)} %get-tuple-element.17.dk_ref, bf16[4,192,32,128]{3,2,1,0:T(8,128)(2,1)} %get-tuple-element.18.dv_ref), custom_call_target="tpu_custom_call" | custom-call | tf_op jit(solution)/shard_map/give/pallas_call | solution.py:454
  192.1 1.3 copy.17
  193.5 0.9 copy.18
  194.3 0.9 copy.19
  (1 shorter events, 0.0 us)
Async XLA Ops:
  121.1 1.6 copy-start

commit v3 on v2

v3 whole, which is shorter than its diff:
```python
import functools

import jax
import jax.numpy as jnp
import numpy as np
from jax import lax
from jax.experimental import pallas as pl
from jax.experimental.pallas import tpu as pltpu
from jax.sharding import Mesh
from jax.sharding import PartitionSpec as P

HD = 128
MiB = 1024 * 1024
ANY = pl.BlockSpec(memory_space=pl.ANY)
VMEM = pl.BlockSpec(memory_space=pltpu.VMEM)
SMEM = pl.BlockSpec(memory_space=pltpu.SMEM)
HBM = pl.BlockSpec(memory_space=pltpu.HBM)


def in_hbm(*arrays):
    return tuple(pltpu.with_memory_space_constraint(a, pltpu.HBM) for a in arrays)


def in_vmem(*arrays):
    return tuple(pltpu.with_memory_space_constraint(a, pltpu.VMEM) for a in arrays)


def place():
    return tuple(lax.axis_index(name) for name in ("y", "z", "x", "c"))


def remote(src, dst, send, recv, where):
    return pltpu.make_async_remote_copy(
        src_ref=src,
        dst_ref=dst,
        send_sem=send,
        recv_sem=recv,
        device_id=where,
        device_id_type=pl.DeviceIdType.MESH,
    )


def greet(nz, nx):
    y, z, x, c = place()
    barrier = pltpu.get_barrier_semaphore()

    def hello(where):
        pl.semaphore_signal(barrier, inc=1, device_id=where, device_id_type=pl.DeviceIdType.MESH)

    @pl.loop(1, nz * nx)
    def _(d):
        hello((y, lax.rem(z + d // nx, nz), lax.rem(x + lax.rem(d, nx), nx), c))

    hello((lax.rem(y + 1, 4), z, x, c))
    hello((lax.rem(y + 3, 4), z, x, c))
    hello((y, z, x, 1 - c))
    pl.semaphore_wait(barrier, nz * nx - 1 + 3)


def contract(a, b, da, db):
    return lax.dot_general(a, b, (((da,), (db,)), ((), ())), preferred_element_type=jnp.float32)


def diagonal(a, b):
    empty = jnp.zeros_like(a)
    return jnp.concatenate(
        [jnp.concatenate([a, empty], axis=1), jnp.concatenate([empty, b], axis=1)], axis=0
    )


def entries_of(i_ref, pair):
    per = i_ref.shape[1]
    return [
        i_ref[s // per, lax.rem(s, per), n] for s in (2 * pair, 2 * pair + 1) for n in (0, 1)
    ]


def rows_of(ref, entries):
    quarters, _, tok, _ = ref.shape
    taken = [ref[:, e].reshape(quarters * tok, HD) for e in entries]
    return jnp.concatenate(
        [jnp.concatenate(taken[:2], axis=0), jnp.concatenate(taken[2:], axis=0)], axis=1
    )


def tokens_of(ref, pair):
    per = ref.shape[1]
    sa, sb = 2 * pair, 2 * pair + 1
    return diagonal(ref[sa // per, lax.rem(sa, per)], ref[sb // per, lax.rem(sb, per)])


def offsets(nz, nx):
    steps = [(dz, dx) for dz in range(nz) for dx in range(nx) if dz or dx]

    def hops(step):
        return min(step[0], nz - step[0]) + min(step[1], nx - step[1])

    return sorted(steps, key=hops)


def bring_kernel(
    nz, nx,
    q_ref, g_ref, k_ref, v_ref, i_ref,
    qh, gh, va, ih, lifted_ref, inverse_ref, ka_hbm,
    ka, i_smem, s_in, r_in, s_y, r_y, s_c, r_c, own,
):
    y, z, x, c = place()
    chips = nz * nx
    rows = k_ref.shape[0]
    part = chips * rows
    quarter = k_ref.shape[1] // 4
    me = z * nx + x
    up, down, far = lax.rem(y + 1, 4), lax.rem(y + 3, 4), lax.rem(y + 2, 4)
    greet(nz, nx)

    def columns(head):
        return pl.ds(pl.multiple_of(head * HD, HD), HD)

    def token_part(ref, head):
        return ref.at[:, pl.ds(pl.multiple_of(y * quarter, quarter), quarter), columns(head)]

    def landing(ref):
        return ref.at[y, pl.ds(c * part + me * rows, rows)]

    def sides(t, head):
        if t < 2:
            return token_part((k_ref, v_ref)[t], head), landing((ka, va)[t])
        if t < 4:
            return (q_ref, g_ref)[t - 2].at[:, :, columns(head)], (qh, gh)[t - 2].at[me]
        return i_ref, ih.at[me]

    def to_chip(t, d):
        pz, px = lax.rem(z + d // nx, nz), lax.rem(x + lax.rem(d, nx), nx)
        return remote(*sides(t, pz * nx + px), s_in.at[t, d], r_in.at[t, d], (y, pz, px, c))

    def keep(t):
        return pltpu.make_async_copy(*sides(t, me), own.at[t])

    def arrived(t):
        @pl.loop(1, chips)
        def _(d):
            to_chip(t, d).wait_recv()

        keep(t).wait()

    def send(t):
        for dz, dx in offsets(nz, nx):
            to_chip(t, dz * nx + dx).start()
        keep(t).start()

    for t in (0, 1, 4, 2):
        send(t)

    def chunk(t, at):
        return (ka, va)[t].at[at, pl.ds(c * part, part)]

    def along_y(t, at, slot, where):
        return remote(
            chunk(t, at), chunk(t, at), s_y.at[t, slot], r_y.at[t, slot], (where, z, x, c)
        )

    def across(t, at, slot):
        return remote(
            chunk(t, at), chunk(t, at), s_c.at[t, slot], r_c.at[t, slot], (y, z, x, 1 - c)
        )

    arrived(0)
    along_y(0, y, 0, up).start()
    along_y(0, y, 1, down).start()
    across(0, y, 0).start()
    arrived(1)
    along_y(1, y, 1, down).start()
    across(1, y, 0).start()
    send(3)

    def all_across(t):
        along_y(t, far, 2, up).wait_recv()
        across(t, far, 3).start()
        for slot in range(4):
            across(t, y, slot).wait_recv()

    arrived(4)
    entry_copy = pltpu.make_async_copy(ih, i_smem, own.at[5])
    entry_copy.start()
    entry_copy.wait()
    along_y(0, down, 0, up).wait_recv()
    along_y(0, down, 2, up).start()
    along_y(1, y, 0, up).start()
    across(0, down, 1).start()
    along_y(0, up, 1, down).wait_recv()
    across(0, up, 2).start()
    along_y(1, up, 1, down).wait_recv()
    along_y(1, up, 2, down).start()
    across(1, up, 2).start()
    all_across(0)
    keep_keys = pltpu.make_async_copy(ka, ka_hbm, own.at[6])
    keep_keys.start()
    arrived(2)

    to_base2 = HD ** -0.5 * float(np.log2(np.e))
    pairs = lifted_ref.shape[0]
    unroll = min(4, pairs)

    def weigh(first, last):
        @pl.loop(first, last)
        def _(step):
            for u in range(unroll):
                p = step * unroll + u
                scores = contract(rows_of(ka, entries_of(i_smem, p)), tokens_of(qh, p), 1, 1)
                lifted = jnp.exp2((scores - jnp.max(scores, axis=0, keepdims=True)) * to_base2)
                inverse_ref[p] = 1.0 / jnp.sum(lifted, axis=0, keepdims=True)
                lifted_ref[p] = lifted.astype(jnp.bfloat16)

    steps = pairs // unroll
    weigh(0, steps // 2)
    along_y(1, down, 0, up).wait_recv()
    across(1, down, 1).start()
    weigh(steps // 2, steps)
    all_across(1)
    arrived(3)
    keep_keys.wait()
    for t in range(5):

        @pl.loop(1, chips)
        def _(d):
            to_chip(t, d).wait_send()

    for t in (0, 1):
        for slot in range(3):
            along_y(t, y, slot, up).wait_send()
        for slot in range(4):
            across(t, y, slot).wait_send()


def bring(nz, nx, query, grad_out, keys, values, entry):
    chips = nz * nx
    rows, tokens, _ = keys.shape
    spans, span_len, _ = query.shape
    bf16 = jnp.bfloat16
    held = pltpu.VMEM((4, 2 * chips * rows, tokens // 4, HD), bf16)
    heads = pltpu.VMEM((chips, spans, span_len, HD), bf16)
    pairs = chips * spans // 2
    dma = pltpu.SemaphoreType.DMA
    return pl.pallas_call(
        functools.partial(bring_kernel, nz, nx),
        name="bring",
        out_shape=(
            heads, heads, held,
            jax.ShapeDtypeStruct((chips,) + entry.shape, jnp.int32),
            pltpu.VMEM((pairs, 2 * tokens, 2 * span_len), bf16),
            pltpu.VMEM((pairs, 1, 2 * span_len), jnp.float32),
            pltpu.HBM(held.shape, bf16),
        ),
        in_specs=[HBM] * 4 + [ANY],
        out_specs=(VMEM,) * 3 + (ANY,) + (VMEM,) * 2 + (HBM,),
        scratch_shapes=[
            pltpu.VMEM(held.shape, bf16),
            pltpu.SMEM((chips,) + entry.shape, jnp.int32),
            dma((5, chips)), dma((5, chips)), dma((2, 3)), dma((2, 3)), dma((2, 4)), dma((2, 4)), dma((7,)),
        ],
        compiler_params=pltpu.CompilerParams(
            collective_id=0, has_side_effects=True, vmem_limit_bytes=14 * MiB
        ),
    )(*in_hbm(query, grad_out, keys, values), entry)


def attend_kernel(
    i_ref, qh, gh, va, lifted_ref, inverse_ref, dscore_ref, dk_low, dv_low, dk, dv
):
    quarters, rows, tok, _ = va.shape
    tokens = quarters * tok
    scaling = HD ** -0.5
    pairs = lifted_ref.shape[0]
    unroll = min(4, pairs)

    def gradients(p):
        entries = entries_of(i_ref, p)
        grads = tokens_of(gh, p)
        dprob = contract(rows_of(va, entries), grads, 1, 1)
        inverse = inverse_ref[p]
        lifted = lifted_ref[p].astype(jnp.float32)
        delta = jnp.sum(lifted * dprob, axis=0, keepdims=True) * inverse
        chance_low = (lifted * inverse).astype(jnp.bfloat16)
        dscore = (lifted * (inverse * scaling) * (dprob - delta)).astype(jnp.bfloat16)
        dscore_ref[p] = dscore
        return entries, contract(dscore, tokens_of(qh, p), 1, 0), contract(chance_low, grads, 1, 0)

    @pl.loop(0, rows)
    def _(r):
        dk[:, r] = jnp.zeros((quarters, tok, HD), jnp.float32)
        dv[:, r] = jnp.zeros((quarters, tok, HD), jnp.float32)

    @pl.loop(0, pairs // unroll)
    def _(step):
        results = [gradients(step * unroll + u) for u in range(unroll)]
        for entries, key_terms, value_terms in results:
            for at, e in enumerate(entries):
                rs = slice(at % 2 * tokens, (at % 2 + 1) * tokens)
                cs = slice(at // 2 * HD, (at // 2 + 1) * HD)
                dk[:, e] += key_terms[rs, cs].reshape(quarters, tok, HD)
                dv[:, e] += value_terms[rs, cs].reshape(quarters, tok, HD)

    @pl.loop(0, rows)
    def _(r):
        dk_low[:, r] = dk[:, r].astype(jnp.bfloat16)
        dv_low[:, r] = dv[:, r].astype(jnp.bfloat16)


def attend(ih, qh, gh, va, lifted, inverse):
    held = pltpu.VMEM(va.shape, jnp.bfloat16)
    work = lifted.size * HD * 2
    return pl.pallas_call(
        attend_kernel,
        name="attend",
        out_shape=(pltpu.VMEM(lifted.shape, jnp.bfloat16), held, held),
        in_specs=[SMEM] + [VMEM] * 5,
        out_specs=(VMEM,) * 3,
        scratch_shapes=[pltpu.VMEM(va.shape, jnp.float32)] * 2,
        input_output_aliases={4: 0, 3: 2},
        compiler_params=pltpu.CompilerParams(vmem_limit_bytes=28 * MiB),
        cost_estimate=pl.CostEstimate(flops=3 * work, bytes_accessed=4 * MiB, transcendentals=0),
    )(ih, *in_vmem(qh, gh, va, lifted, inverse))


def give_kernel(
    nz, nx,
    i_ref, ka_hbm, dscore_ref, dk_ref, dv_ref,
    gq, gk, gv,
    ka, dq_ref, other, total, passed, arrived,
    s_q, r_q, s_out, r_out, s_c, r_c, s_f, r_f, s_y, r_y, own_q, own_out, own_k,
):
    y, z, x, c = place()
    chips = nz * nx
    part = chips * (gk.shape[0])
    rows = part // chips
    band = nx * rows
    me = z * nx + x
    up, down, far = lax.rem(y + 1, 4), lax.rem(y + 3, 4), lax.rem(y + 2, 4)
    pair = (dk_ref, dv_ref)
    outs = (gk, gv)
    greet(nz, nx)

    at = (far, up, down, y)
    bands = sorted(range(nz), key=lambda dz: -min(dz, nz - dz))

    def first_row(dz):
        return lax.rem(z + dz, nz) * band

    def across(t, slot, dz):
        return remote(
            pair[t].at[at[slot], pl.ds((1 - c) * part + first_row(dz), band)],
            other.at[slot, t, dz],
            s_c.at[slot, t, dz], r_c.at[slot, t, dz], (y, z, x, 1 - c),
        )

    def mine(t, slot, dz):
        return pair[t].at[at[slot], pl.ds(c * part + first_row(dz), band)]

    for dz in bands:
        for slot in range(4):
            for t in (0, 1):
                across(t, slot, dz).start()

    def columns(head):
        return pl.ds(pl.multiple_of(head * HD, HD), HD)

    def chip(d):
        pz, px = lax.rem(z + d // nx, nz), lax.rem(x + lax.rem(d, nx), nx)
        return pz * nx + px, (y, pz, px, c)

    def query_out(d):
        head, where = chip(d)
        return remote(dq_ref.at[head], gq.at[:, :, columns(me)], s_q.at[d], r_q.at[d], where)

    def key_out(d, t):
        _, where = chip(d)
        px = lax.rem(x + lax.rem(d, nx), nx)
        return remote(
            total.at[3, t, d // nx, pl.ds(px * rows, rows)], outs[t].at[:, :, columns(me)],
            s_out.at[t, d], r_out.at[t, d], where,
        )

    def key_own(t):
        return pltpu.make_async_copy(
            total.at[3, t, 0, pl.ds(x * rows, rows)], outs[t].at[:, :, columns(me)], own_out.at[t]
        )

    query_own = pltpu.make_async_copy(dq_ref.at[me], gq.at[:, :, columns(me)], own_q)
    keys_in = pltpu.make_async_copy(ka_hbm, ka, own_k)
    keys_in.start()
    pairs = dscore_ref.shape[0]
    per = dq_ref.shape[1]
    span_len = dq_ref.shape[2]
    unroll = min(4, pairs)

    def queries():
        keys_in.wait()

        @pl.loop(0, pairs // unroll)
        def _(step):
            for u in range(unroll):
                p = step * unroll + u
                both = contract(dscore_ref[p], rows_of(ka, entries_of(i_ref, p)), 0, 0)
                sa, sb = 2 * p, 2 * p + 1
                dq_ref[sa // per, lax.rem(sa, per)] = both[:span_len, :HD].astype(jnp.bfloat16)
                dq_ref[sb // per, lax.rem(sb, per)] = both[span_len:, HD:].astype(jnp.bfloat16)

        query_own.start()
        for dz, dx in offsets(nz, nx):
            query_out(dz * nx + dx).start()

    def f32(a):
        return a.astype(jnp.float32)

    def add(dst, *terms):
        @pl.loop(0, band // rows)
        def _(i):
            rs = pl.ds(i * rows, rows)
            sums = f32(terms[0][rs])
            for term in terms[1:]:
                sums = sums + f32(term[rs])
            dst[rs] = sums.astype(jnp.bfloat16)

    def both_cores(t, slot, dz):
        across(t, slot, dz).wait_recv()
        return mine(t, slot, dz), other.at[slot, t, dz]

    def far_copy(t, dz):
        return remote(
            total.at[0, t, dz], passed.at[t, dz], s_f.at[t, dz], r_f.at[t, dz],
            ((up, down)[t], z, x, c),
        )

    def near_copy(t, slot, dz):
        return remote(
            total.at[slot, t, dz], arrived.at[slot - 1, t, dz],
            s_y.at[slot - 1, t, dz], r_y.at[slot - 1, t, dz],
            ((up, down)[slot - 1], z, x, c),
        )

    def direct(dz):
        for t in (0, 1):
            add(total.at[0, t, dz], *both_cores(t, 0, dz))
            far_copy(t, dz).start()
        for t, slot in ((1, 1), (0, 2)):
            add(total.at[slot, t, dz], *both_cores(t, slot, dz))
            near_copy(t, slot, dz).start()

    def merged(dz):
        for t, slot in ((0, 1), (1, 2)):
            terms = both_cores(t, slot, dz)
            far_copy(t, dz).wait_recv()
            add(total.at[slot, t, dz], *terms, passed.at[t, dz])
            near_copy(t, slot, dz).start()

    def final(dz):
        for t in (0, 1):
            terms = both_cores(t, 3, dz)
            near_copy(t, 1, dz).wait_recv()
            near_copy(t, 2, dz).wait_recv()
            add(total.at[3, t, dz], *terms, arrived.at[0, t, dz], arrived.at[1, t, dz])
            for dx in range(nx):
                if dz or dx:
                    key_out(dz * nx + dx, t).start()
                else:
                    key_own(t).start()

    for step in range(nz + 2):
        if step < nz:
            direct(bands[step])
        if step == min(1, nz - 1):
            queries()
        if 1 <= step < nz + 1:
            merged(bands[step - 1])
        if step >= 2:
            final(bands[step - 2])

    @pl.loop(1, chips)
    def _(d):
        query_out(d).wait()
        for t in (0, 1):
            key_out(d, t).wait()

    query_own.wait()
    for t in (0, 1):
        key_own(t).wait()

        @pl.loop(0, nz)
        def _(dz):
            far_copy(t, dz).wait_send()
            for slot in range(4):
                across(t, slot, dz).wait_send()
            for slot in (1, 2):
                near_copy(t, slot, dz).wait_send()


def give(nz, nx, spans, ih, ka, dscore, dk, dv):
    chips = nz * nx
    _, all_rows, tok, _ = dk.shape
    part = all_rows // 2
    band = part // nz
    span_len = dscore.shape[2] // 2
    bf16 = jnp.bfloat16
    dma = pltpu.SemaphoreType.DMA
    row_out = pltpu.VMEM((part // chips, tok, chips * HD), bf16)
    return pl.pallas_call(
        functools.partial(give_kernel, nz, nx),
        name="give",
        out_shape=(pltpu.VMEM((spans, span_len, chips * HD), bf16), row_out, row_out),
        in_specs=[SMEM, HBM] + [VMEM] * 3,
        out_specs=(ANY,) * 3,
        scratch_shapes=[
            pltpu.VMEM(ka.shape, bf16),
            pltpu.VMEM((chips, spans, span_len, HD), bf16),
            pltpu.VMEM((4, 2, nz, band, tok, HD), bf16),
            pltpu.VMEM((4, 2, nz, band, tok, HD), bf16),
            pltpu.VMEM((2, nz, band, tok, HD), bf16),
            pltpu.VMEM((2, 2, nz, band, tok, HD), bf16),
            dma((chips,)), dma((chips,)), dma((2, chips)), dma((2, chips)),
            dma((4, 2, nz)), dma((4, 2, nz)), dma((2, nz)), dma((2, nz)),
            dma((2, 2, nz)), dma((2, 2, nz)), dma, dma((2,)), dma,
        ],
        compiler_params=pltpu.CompilerParams(
            collective_id=1, has_side_effects=True, vmem_limit_bytes=32 * MiB
        ),
    )(ih, *in_hbm(ka), *in_vmem(dscore, dk, dv))


def on_device(nz, nx, query, grad_out, keys, values, owner_list, row_list):
    chips = nz * nx
    rows = keys.shape[0]
    entry = lax.rem(owner_list, 2) * (chips * rows) + (owner_list // 2) * rows + row_list
    entry = jnp.pad(entry, ((0, 0), (0, HD - entry.shape[1])))
    qh, gh, va, ih, lifted, inverse, ka = bring(
        nz, nx, query, grad_out, keys, values, entry
    )
    dscore, dk, dv = attend(ih, qh, gh, va, lifted, inverse)
    return give(nz, nx, query.shape[0], ih, ka, dscore, dk, dv)


def solution(mesh):
    groups, retr = mesh.devices.shape
    nx = 4 if retr == 32 else 2
    nz = retr // (2 * nx)
    fine = Mesh(mesh.devices.reshape(groups, nz, nx, 2), ("y", "z", "x", "c"))
    all_axes = ("y", "z", "x", "c")
    owner = ("z", "x", "c")
    return jax.shard_map(
        functools.partial(on_device, nz, nx),
        mesh=fine,
        in_specs=(
            P(all_axes, None, None),
            P(all_axes, None, None),
            P(owner, None, None),
            P(owner, None, None),
            P(all_axes, None),
            P(all_axes, None),
        ),
        out_specs=(P(all_axes, None, None), P(owner, "y", None), P(owner, "y", None)),
        check_vma=False,
    )
```

time: 195 us -> 178 us (0.913)
  Pallas kernels: 188 us -> 173 us
  local copies, waits for them, and re-layouts: 6.77 us -> 4.59 us
    pallas_call x1, Pallas kernels: 40.4 us -> 23.9 us  [attend(): pl.pallas_call(attend_kernel, name='attend', out_shape=(pltpu.VMEM(lifted...]
    pallas_call x1, Pallas kernels: 77.9 us -> 80.2 us  [bring(): pl.pallas_call(functools.partial(bring_kernel, nz, nx), name='bring', out...]
    unnamed x7 -> x5, local copies, waits for them, and re-layouts: 6.17 us -> 4.59 us
where the time goes in v3:
time: 178 us
  Pallas kernels  173 us (97%)
  local copies, waits for them, and re-layouts  4.59 us (3%)
    pallas_call x1, Pallas kernels, bring(): pl.pallas_call(functools.partial(bring_kernel, nz, nx), name='bring', out...  80.2 us
    pallas_call x1, Pallas kernels, give(): pl.pallas_call(functools.partial(give_kernel, nz, nx), name='give', out_s...  69 us
    pallas_call x1, Pallas kernels, attend(): pl.pallas_call(attend_kernel, name='attend', out_shape=(pltpu.VMEM(lifted...  23.9 us
    unnamed x5, local copies, waits for them, and re-layouts  4.59 us

profile of v3, /device:TPU:1, one launch (start us, length us, event | category | flops | bytes accessed | tf_op | source)
XLA Modules:
  0.0 178.3 jit_solution(13610111864926566713)
XLA Ops:
  0.6 0.8 copy.11
  1.4 0.8 copy.15
  2.2 80.2 %bring.1 = (bf16[16,8,64,128]{3,2,1,0:T(8,128)(2,1)S(1)}, bf16[16,8,64,128]{3,2,1,0:T(8,128)(2,1)S(1)}, bf16[4,192,32,128]{3,2,1,0:T(8,128)(2,1)S(1)}, s32[16,8,...) custom-call(bf16[8,64,2048]{2,1,0:T(8,128)(2,1)} %q_ref.1, ...), custom_call_target="tpu_custom_call" | custom-call | tf_op jit(solution)/shard_map/bring/pallas_call | solution.py:244
  82.4 23.9 %attend.1 = (bf16[64,256,128]{2,1,0:T(8,128)(2,1)S(1)}, bf16[4,192,32,128]{3,2,1,0:T(8,128)(2,1)S(1)}, bf16[4,192,32,128]{3,2,1,0:T(8,128)(2,1)S(1)}) custom-call(s32[16,8,128]{2,1,0:T(8,128)S(1)} %get-tuple-element.13.i_ref, bf16[16,8,64,128]{3,2,1,0:T(8,128)(2,1)S(1)} %get-tuple-element.15.qh, ...), custom_call_target="tpu_custom_call", output_to_operand_aliasing={{0}: (4, {}), {2}: (3, {})} | custom-call | flops 1610612736 | bytes 4194304 | tf_op jit(solution)/shard_map/attend/pallas_call | solution.py:312
  106.3 69.0 %give.1 = (bf16[8,64,2048]{2,1,0:T(8,128)(2,1)S(1)}, bf16[6,32,2048]{2,1,0:T(8,128)(2,1)S(1)}, bf16[6,32,2048]{2,1,0:T(8,128)(2,1)S(1)}) custom-call(s32[16,8,128]{2,1,0:T(8,128)S(1)} %get-tuple-element.13.i_ref, bf16[4,192,32,128]{3,2,1,0:T(8,128)(2,1)} %get-tuple-element.14.ka_hbm, bf16[64,256,128]{2,1,0:T(8,128)(2,1)S(1)} %get-tuple-element.20.dscore_ref, ...), custom_call_target="tpu_custom_call" | custom-call | tf_op jit(solution)/shard_map/give/pallas_call | solution.py:506
  175.2 1.3 copy.21
  176.5 0.9 copy.22
  177.4 0.9 copy.23
  (2 shorter events, 0.0 us)

commit v4 on v3

--- a/solution.py
+++ b/solution.py
@@ -271,7 +271,13 @@
     tokens = quarters * tok
     scaling = HD ** -0.5
     pairs = lifted_ref.shape[0]
-    unroll = min(4, pairs)
+    unroll = min(8, pairs)
+
+    def add(sums, entries, terms):
+        for at, e in enumerate(entries):
+            rs = slice(at % 2 * tokens, (at % 2 + 1) * tokens)
+            cs = slice(at // 2 * HD, (at // 2 + 1) * HD)
+            sums[:, e] += terms[rs, cs].reshape(quarters, tok, HD)
 
     def gradients(p):
         entries = entries_of(i_ref, p)
@@ -283,7 +289,7 @@
         chance_low = (lifted * inverse).astype(jnp.bfloat16)
         dscore = (lifted * (inverse * scaling) * (dprob - delta)).astype(jnp.bfloat16)
         dscore_ref[p] = dscore
-        return entries, contract(dscore, tokens_of(qh, p), 1, 0), contract(chance_low, grads, 1, 0)
+        return entries, contract(chance_low, grads, 1, 0)
 
     @pl.loop(0, rows)
     def _(r):
@@ -293,12 +299,19 @@
     @pl.loop(0, pairs // unroll)
     def _(step):
         results = [gradients(step * unroll + u) for u in range(unroll)]
-        for entries, key_terms, value_terms in results:
-            for at, e in enumerate(entries):
-                rs = slice(at % 2 * tokens, (at % 2 + 1) * tokens)
-                cs = slice(at // 2 * HD, (at // 2 + 1) * HD)
-                dk[:, e] += key_terms[rs, cs].reshape(quarters, tok, HD)
-                dv[:, e] += value_terms[rs, cs].reshape(quarters, tok, HD)
+        for entries, value_terms in results:
+            add(dv, entries, value_terms)
+
+    @pl.loop(0, pairs // unroll)
+    def _(step):
+        results = []
+        for u in range(unroll):
+            p = step * unroll + u
+            results.append(
+                (entries_of(i_ref, p), contract(dscore_ref[p], tokens_of(qh, p), 1, 0))
+            )
+        for entries, key_terms in results:
+            add(dk, entries, key_terms)
 
     @pl.loop(0, rows)
     def _(r):

time: 178 us -> 171 us (0.961)
  Pallas kernels: 173 us -> 166 us
    pallas_call x1, Pallas kernels: 23.9 us -> 16.6 us  [attend(): pl.pallas_call(attend_kernel, name='attend', out_shape=(pltpu.VMEM(lifted...]
where the time goes in v4:
time: 171 us
  Pallas kernels  166 us (97%)
  local copies, waits for them, and re-layouts  4.59 us (3%)
    pallas_call x1, Pallas kernels, bring(): pl.pallas_call(functools.partial(bring_kernel, nz, nx), name='bring', out...  80.2 us
    pallas_call x1, Pallas kernels, give(): pl.pallas_call(functools.partial(give_kernel, nz, nx), name='give', out_s...  68.9 us
    pallas_call x1, Pallas kernels, attend(): pl.pallas_call(attend_kernel, name='attend', out_shape=(pltpu.VMEM(lifted...  16.6 us
    unnamed x5, local copies, waits for them, and re-layouts  4.59 us

profile of v4, /device:TPU:1, one launch (start us, length us, event | category | flops | bytes accessed | tf_op | source)
XLA Modules:
  0.0 170.9 jit_solution(2074384211941926667)
XLA Ops:
  0.6 0.8 copy.11
  1.4 0.8 copy.15
  2.2 80.2 %bring.1 = (bf16[16,8,64,128]{3,2,1,0:T(8,128)(2,1)S(1)}, bf16[16,8,64,128]{3,2,1,0:T(8,128)(2,1)S(1)}, bf16[4,192,32,128]{3,2,1,0:T(8,128)(2,1)S(1)}, s32[16,8,...) custom-call(bf16[8,64,2048]{2,1,0:T(8,128)(2,1)} %q_ref.1, ...), custom_call_target="tpu_custom_call" | custom-call | tf_op jit(solution)/shard_map/bring/pallas_call | solution.py:244
  82.4 16.6 %attend.1 = (bf16[64,256,128]{2,1,0:T(8,128)(2,1)S(1)}, bf16[4,192,32,128]{3,2,1,0:T(8,128)(2,1)S(1)}, bf16[4,192,32,128]{3,2,1,0:T(8,128)(2,1)S(1)}) custom-call(s32[16,8,128]{2,1,0:T(8,128)S(1)} %get-tuple-element.13.i_ref, bf16[16,8,64,128]{3,2,1,0:T(8,128)(2,1)S(1)} %get-tuple-element.15.qh, ...), custom_call_target="tpu_custom_call", output_to_operand_aliasing={{0}: (4, {}), {2}: (3, {})} | custom-call | flops 1610612736 | bytes 4194304 | tf_op jit(solution)/shard_map/attend/pallas_call | solution.py:325
  99.0 68.9 %give.1 = (bf16[8,64,2048]{2,1,0:T(8,128)(2,1)S(1)}, bf16[6,32,2048]{2,1,0:T(8,128)(2,1)S(1)}, bf16[6,32,2048]{2,1,0:T(8,128)(2,1)S(1)}) custom-call(s32[16,8,128]{2,1,0:T(8,128)S(1)} %get-tuple-element.13.i_ref, bf16[4,192,32,128]{3,2,1,0:T(8,128)(2,1)} %get-tuple-element.14.ka_hbm, bf16[64,256,128]{2,1,0:T(8,128)(2,1)S(1)} %get-tuple-element.20.dscore_ref, ...), custom_call_target="tpu_custom_call" | custom-call | tf_op jit(solution)/shard_map/give/pallas_call | solution.py:519
  167.9 1.3 copy.21
  169.2 0.9 copy.22
  170.1 0.9 copy.23
  (2 shorter events, 0.0 us)

commit v5 on v4

--- a/solution.py
+++ b/solution.py
@@ -68,10 +68,9 @@
     )
 
 
-def entries_of(i_ref, pair):
-    per = i_ref.shape[1]
+def entries_of(i_ref, pair, per):
     return [
-        i_ref[s // per, lax.rem(s, per), n] for s in (2 * pair, 2 * pair + 1) for n in (0, 1)
+        i_ref[s // per, n, lax.rem(s, per)] for s in (2 * pair, 2 * pair + 1) for n in (0, 1)
     ]
 
 
@@ -100,9 +99,9 @@
 
 def bring_kernel(
     nz, nx,
-    q_ref, g_ref, k_ref, v_ref, i_ref,
+    q_ref, g_ref, k_ref, v_ref, owner_ref, row_ref,
     qh, gh, va, ih, lifted_ref, inverse_ref, ka_hbm,
-    ka, i_smem, s_in, r_in, s_y, r_y, s_c, r_c, own,
+    ka, i_ref, i_smem, s_in, r_in, s_y, r_y, s_c, r_c, own,
 ):
     y, z, x, c = place()
     chips = nz * nx
@@ -112,6 +111,11 @@
     me = z * nx + x
     up, down, far = lax.rem(y + 1, 4), lax.rem(y + 3, 4), lax.rem(y + 2, 4)
     greet(nz, nx)
+
+    owners = owner_ref[...]
+    entries = (owners & 1) * part + (owners >> 1) * rows + row_ref[...]
+    i_ref[...] = jnp.zeros_like(i_ref)
+    i_ref[: entries.shape[0], : entries.shape[1]] = entries
 
     def columns(head):
         return pl.ds(pl.multiple_of(head * HD, HD), HD)
@@ -206,7 +210,7 @@
         def _(step):
             for u in range(unroll):
                 p = step * unroll + u
-                scores = contract(rows_of(ka, entries_of(i_smem, p)), tokens_of(qh, p), 1, 1)
+                scores = contract(rows_of(ka, entries_of(i_smem, p, qh.shape[1])), tokens_of(qh, p), 1, 1)
                 lifted = jnp.exp2((scores - jnp.max(scores, axis=0, keepdims=True)) * to_base2)
                 inverse_ref[p] = 1.0 / jnp.sum(lifted, axis=0, keepdims=True)
                 lifted_ref[p] = lifted.astype(jnp.bfloat16)
@@ -232,7 +236,7 @@
             across(t, y, slot).wait_send()
 
 
-def bring(nz, nx, query, grad_out, keys, values, entry):
+def bring(nz, nx, query, grad_out, keys, values, owner_list, row_list):
     chips = nz * nx
     rows, tokens, _ = keys.shape
     spans, span_len, _ = query.shape
@@ -240,28 +244,30 @@
     held = pltpu.VMEM((4, 2 * chips * rows, tokens // 4, HD), bf16)
     heads = pltpu.VMEM((chips, spans, span_len, HD), bf16)
     pairs = chips * spans // 2
+    listed = (8, HD)
     dma = pltpu.SemaphoreType.DMA
     return pl.pallas_call(
         functools.partial(bring_kernel, nz, nx),
         name="bring",
         out_shape=(
             heads, heads, held,
-            jax.ShapeDtypeStruct((chips,) + entry.shape, jnp.int32),
+            jax.ShapeDtypeStruct((chips,) + listed, jnp.int32),
             pltpu.VMEM((pairs, 2 * tokens, 2 * span_len), bf16),
             pltpu.VMEM((pairs, 1, 2 * span_len), jnp.float32),
             pltpu.HBM(held.shape, bf16),
         ),
-        in_specs=[HBM] * 4 + [ANY],
+        in_specs=[HBM] * 4 + [VMEM] * 2,
         out_specs=(VMEM,) * 3 + (ANY,) + (VMEM,) * 2 + (HBM,),
         scratch_shapes=[
             pltpu.VMEM(held.shape, bf16),
-            pltpu.SMEM((chips,) + entry.shape, jnp.int32),
+            pltpu.VMEM(listed, jnp.int32),
+            pltpu.SMEM((chips,) + listed, jnp.int32),
             dma((5, chips)), dma((5, chips)), dma((2, 3)), dma((2, 3)), dma((2, 4)), dma((2, 4)), dma((7,)),
         ],
         compiler_params=pltpu.CompilerParams(
             collective_id=0, has_side_effects=True, vmem_limit_bytes=14 * MiB
         ),
-    )(*in_hbm(query, grad_out, keys, values), entry)
+    )(*in_hbm(query, grad_out, keys, values), owner_list.T, row_list.T)
 
 
 def attend_kernel(
@@ -280,7 +286,7 @@
             sums[:, e] += terms[rs, cs].reshape(quarters, tok, HD)
 
     def gradients(p):
-        entries = entries_of(i_ref, p)
+        entries = entries_of(i_ref, p, qh.shape[1])
         grads = tokens_of(gh, p)
         dprob = contract(rows_of(va, entries), grads, 1, 1)
         inverse = inverse_ref[p]
@@ -308,7 +314,7 @@
         for u in range(unroll):
             p = step * unroll + u
             results.append(
-                (entries_of(i_ref, p), contract(dscore_ref[p], tokens_of(qh, p), 1, 0))
+                (entries_of(i_ref, p, qh.shape[1]), contract(dscore_ref[p], tokens_of(qh, p), 1, 0))
             )
         for entries, key_terms in results:
             add(dk, entries, key_terms)
@@ -344,9 +350,8 @@
 ):
     y, z, x, c = place()
     chips = nz * nx
-    part = chips * (gk.shape[0])
-    rows = part // chips
-    band = nx * rows
+    rows = gk.shape[0]
+    half = rows // 2
     me = z * nx + x
     up, down, far = lax.rem(y + 1, 4), lax.rem(y + 3, 4), lax.rem(y + 2, 4)
     pair = (dk_ref, dv_ref)
@@ -354,25 +359,22 @@
     greet(nz, nx)
 
     at = (far, up, down, y)
-    bands = sorted(range(nz), key=lambda dz: -min(dz, nz - dz))
-
-    def first_row(dz):
-        return lax.rem(z + dz, nz) * band
-
-    def across(t, slot, dz):
+    bands = [(dz, h) for dz in sorted(range(nz), key=lambda dz: -min(dz, nz - dz)) for h in (0, 1)]
+
+    def rows_at(t, slot, dz, h, core):
+        first = core * chips + lax.rem(z + dz, nz) * nx
+        return pair[t].at[at[slot], pl.ds(first, nx), pl.ds(h * half, half)]
+
+    def across(t, slot, dz, h):
         return remote(
-            pair[t].at[at[slot], pl.ds((1 - c) * part + first_row(dz), band)],
-            other.at[slot, t, dz],
-            s_c.at[slot, t, dz], r_c.at[slot, t, dz], (y, z, x, 1 - c),
+            rows_at(t, slot, dz, h, 1 - c), other.at[slot, t, dz, h],
+            s_c.at[slot, t, dz, h], r_c.at[slot, t, dz, h], (y, z, x, 1 - c),
         )
 
-    def mine(t, slot, dz):
-        return pair[t].at[at[slot], pl.ds(c * part + first_row(dz), band)]
-
-    for dz in bands:
+    for dz, h in bands:
         for slot in range(4):
             for t in (0, 1):
-                across(t, slot, dz).start()
+                across(t, slot, dz, h).start()
 
     def columns(head):
         return pl.ds(pl.multiple_of(head * HD, HD), HD)
@@ -385,17 +387,18 @@
         head, where = chip(d)
         return remote(dq_ref.at[head], gq.at[:, :, columns(me)], s_q.at[d], r_q.at[d], where)
 
-    def key_out(d, t):
+    def key_out(d, t, h):
         _, where = chip(d)
         px = lax.rem(x + lax.rem(d, nx), nx)
         return remote(
-            total.at[3, t, d // nx, pl.ds(px * rows, rows)], outs[t].at[:, :, columns(me)],
-            s_out.at[t, d], r_out.at[t, d], where,
+            total.at[3, t, d // nx, h, px], outs[t].at[pl.ds(h * half, half), :, columns(me)],
+            s_out.at[t, h, d], r_out.at[t, h, d], where,
         )
 
-    def key_own(t):
+    def key_own(t, h):
         return pltpu.make_async_copy(
-            total.at[3, t, 0, pl.ds(x * rows, rows)], outs[t].at[:, :, columns(me)], own_out.at[t]
+            total.at[3, t, 0, h, x], outs[t].at[pl.ds(h * half, half), :, columns(me)],
+            own_out.at[t, h],
         )
 
     query_own = pltpu.make_async_copy(dq_ref.at[me], gq.at[:, :, columns(me)], own_q)
@@ -413,7 +416,7 @@
         def _(step):
             for u in range(unroll):
                 p = step * unroll + u
-                both = contract(dscore_ref[p], rows_of(ka, entries_of(i_ref, p)), 0, 0)
+                both = contract(dscore_ref[p], rows_of(ka, entries_of(i_ref, p, per)), 0, 0)
                 sa, sb = 2 * p, 2 * p + 1
                 dq_ref[sa // per, lax.rem(sa, per)] = both[:span_len, :HD].astype(jnp.bfloat16)
                 dq_ref[sb // per, lax.rem(sb, per)] = both[span_len:, HD:].astype(jnp.bfloat16)
@@ -426,95 +429,101 @@
         return a.astype(jnp.float32)
 
     def add(dst, *terms):
-        @pl.loop(0, band // rows)
+        @pl.loop(0, nx)
         def _(i):
-            rs = pl.ds(i * rows, rows)
-            sums = f32(terms[0][rs])
+            sums = f32(terms[0][i])
             for term in terms[1:]:
-                sums = sums + f32(term[rs])
-            dst[rs] = sums.astype(jnp.bfloat16)
-
-    def both_cores(t, slot, dz):
-        across(t, slot, dz).wait_recv()
-        return mine(t, slot, dz), other.at[slot, t, dz]
-
-    def far_copy(t, dz):
+                sums = sums + f32(term[i])
+            dst[i] = sums.astype(jnp.bfloat16)
+
+    def both_cores(t, slot, dz, h):
+        across(t, slot, dz, h).wait_recv()
+        return rows_at(t, slot, dz, h, c), other.at[slot, t, dz, h]
+
+    def far_copy(t, dz, h):
         return remote(
-            total.at[0, t, dz], passed.at[t, dz], s_f.at[t, dz], r_f.at[t, dz],
+            total.at[0, t, dz, h], passed.at[t, dz, h], s_f.at[t, dz, h], r_f.at[t, dz, h],
             ((up, down)[t], z, x, c),
         )
 
-    def near_copy(t, slot, dz):
+    def near_copy(t, slot, dz, h):
         return remote(
-            total.at[slot, t, dz], arrived.at[slot - 1, t, dz],
-            s_y.at[slot - 1, t, dz], r_y.at[slot - 1, t, dz],
+            total.at[slot, t, dz, h], arrived.at[slot - 1, t, dz, h],
+            s_y.at[slot - 1, t, dz, h], r_y.at[slot - 1, t, dz, h],
             ((up, down)[slot - 1], z, x, c),
         )
 
-    def direct(dz):
+    def direct(dz, h):
         for t in (0, 1):
-            add(total.at[0, t, dz], *both_cores(t, 0, dz))
-            far_copy(t, dz).start()
+            add(total.at[0, t, dz, h], *both_cores(t, 0, dz, h))
+            far_copy(t, dz, h).start()
         for t, slot in ((1, 1), (0, 2)):
-            add(total.at[slot, t, dz], *both_cores(t, slot, dz))
-            near_copy(t, slot, dz).start()
-
-    def merged(dz):
+            add(total.at[slot, t, dz, h], *both_cores(t, slot, dz, h))
+            near_copy(t, slot, dz, h).start()
+
+    def merged(dz, h):
         for t, slot in ((0, 1), (1, 2)):
-            terms = both_cores(t, slot, dz)
-            far_copy(t, dz).wait_recv()
-            add(total.at[slot, t, dz], *terms, passed.at[t, dz])
-            near_copy(t, slot, dz).start()
-
-    def final(dz):
+            terms = both_cores(t, slot, dz, h)
+            far_copy(t, dz, h).wait_recv()
+            add(total.at[slot, t, dz, h], *terms, passed.at[t, dz, h])
+            near_copy(t, slot, dz, h).start()
+
+    def final(dz, h):
         for t in (0, 1):
-            terms = both_cores(t, 3, dz)
-            near_copy(t, 1, dz).wait_recv()
-            near_copy(t, 2, dz).wait_recv()
-            add(total.at[3, t, dz], *terms, arrived.at[0, t, dz], arrived.at[1, t, dz])
+            terms = both_cores(t, 3, dz, h)
+            near_copy(t, 1, dz, h).wait_recv()
+            near_copy(t, 2, dz, h).wait_recv()
+            add(total.at[3, t, dz, h], *terms, arrived.at[0, t, dz, h], arrived.at[1, t, dz, h])
             for dx in range(nx):
                 if dz or dx:
-                    key_out(dz * nx + dx, t).start()
+                    key_out(dz * nx + dx, t, h).start()
                 else:
-                    key_own(t).start()
-
-    for step in range(nz + 2):
-        if step < nz:
-            direct(bands[step])
-        if step == min(1, nz - 1):
+                    key_own(t, h).start()
+
+    lag = 2
+    for step in range(len(bands) + 2 * lag):
+        if step < len(bands):
+            direct(*bands[step])
+        if step == 2:
             queries()
-        if 1 <= step < nz + 1:
-            merged(bands[step - 1])
-        if step >= 2:
-            final(bands[step - 2])
+        if lag <= step < len(bands) + lag:
+            merged(*bands[step - lag])
+        if step >= 2 * lag:
+            final(*bands[step - 2 * lag])
 
     @pl.loop(1, chips)
     def _(d):
         query_out(d).wait()
         for t in (0, 1):
-            key_out(d, t).wait()
+            for h in (0, 1):
+                key_out(d, t, h).wait()
 
     query_own.wait()
     for t in (0, 1):
-        key_own(t).wait()
-
-        @pl.loop(0, nz)
-        def _(dz):
-            far_copy(t, dz).wait_send()
-            for slot in range(4):
-                across(t, slot, dz).wait_send()
-            for slot in (1, 2):
-                near_copy(t, slot, dz).wait_send()
+        for h in (0, 1):
+            key_own(t, h).wait()
+
+            @pl.loop(0, nz)
+            def _(dz):
+                far_copy(t, dz, h).wait_send()
+                for slot in range(4):
+                    across(t, slot, dz, h).wait_send()
+                for slot in (1, 2):
+                    near_copy(t, slot, dz, h).wait_send()
 
 
 def give(nz, nx, spans, ih, ka, dscore, dk, dv):
     chips = nz * nx
     _, all_rows, tok, _ = dk.shape
     part = all_rows // 2
-    band = part // nz
+    rows = part // chips
+    piece = (nz, 2, nx, rows // 2, tok, HD)
     span_len = dscore.shape[2] // 2
     bf16 = jnp.bfloat16
     dma = pltpu.SemaphoreType.DMA
+    def split(sums):
+        return sums.reshape(4, 2 * chips, rows, tok, HD)
+
     row_out = pltpu.VMEM((part // chips, tok, chips * HD), bf16)
     return pl.pallas_call(
         functools.partial(give_kernel, nz, nx),
@@ -525,30 +534,49 @@
         scratch_shapes=[
             pltpu.VMEM(ka.shape, bf16),
             pltpu.VMEM((chips, spans, span_len, HD), bf16),
-            pltpu.VMEM((4, 2, nz, band, tok, HD), bf16),
-            pltpu.VMEM((4, 2, nz, band, tok, HD), bf16),
-            pltpu.VMEM((2, nz, band, tok, HD), bf16),
-            pltpu.VMEM((2, 2, nz, band, tok, HD), bf16),
-            dma((chips,)), dma((chips,)), dma((2, chips)), dma((2, chips)),
-            dma((4, 2, nz)), dma((4, 2, nz)), dma((2, nz)), dma((2, nz)),
-            dma((2, 2, nz)), dma((2, 2, nz)), dma, dma((2,)), dma,
+            pltpu.VMEM((4, 2) + piece, bf16),
+            pltpu.VMEM((4, 2) + piece, bf16),
+            pltpu.VMEM((2,) + piece, bf16),
+            pltpu.VMEM((2, 2) + piece, bf16),
+            dma((chips,)), dma((chips,)), dma((2, 2, chips)), dma((2, 2, chips)),
+            dma((4, 2, nz, 2)), dma((4, 2, nz, 2)), dma((2, nz, 2)), dma((2, nz, 2)),
+            dma((2, 2, nz, 2)), dma((2, 2, nz, 2)), dma, dma((2, 2)), dma,
         ],
         compiler_params=pltpu.CompilerParams(
             collective_id=1, has_side_effects=True, vmem_limit_bytes=32 * MiB
         ),
-    )(ih, *in_hbm(ka), *in_vmem(dscore, dk, dv))
+    )(ih, *in_hbm(ka), *in_vmem(dscore, split(dk), split(dv)))
+
+
+def write_kernel(*refs):
+    count = (len(refs) - 1) // 2
+    copies = [
+        pltpu.make_async_copy(refs[i], refs[count + i], refs[-1].at[i]) for i in range(count)
+    ]
+    for copy in copies:
+        copy.start()
+    for copy in copies:
+        copy.wait()
+
+
+def write(*arrays):
+    return pl.pallas_call(
+        write_kernel,
+        name="write",
+        out_shape=tuple(pltpu.HBM(a.shape, a.dtype) for a in arrays),
+        in_specs=[VMEM] * len(arrays),
+        out_specs=(HBM,) * len(arrays),
+        scratch_shapes=[pltpu.SemaphoreType.DMA((len(arrays),))],
+        compiler_params=pltpu.CompilerParams(vmem_limit_bytes=8 * MiB),
+    )(*in_vmem(*arrays))
 
 
 def on_device(nz, nx, query, grad_out, keys, values, owner_list, row_list):
-    chips = nz * nx
-    rows = keys.shape[0]
-    entry = lax.rem(owner_list, 2) * (chips * rows) + (owner_list // 2) * rows + row_list
-    entry = jnp.pad(entry, ((0, 0), (0, HD - entry.shape[1])))
     qh, gh, va, ih, lifted, inverse, ka = bring(
-        nz, nx, query, grad_out, keys, values, entry
+        nz, nx, query, grad_out, keys, values, owner_list, row_list
     )
     dscore, dk, dv = attend(ih, qh, gh, va, lifted, inverse)
-    return give(nz, nx, query.shape[0], ih, ka, dscore, dk, dv)
+    return write(*give(nz, nx, query.shape[0], ih, ka, dscore, dk, dv))
 
 
 def solution(mesh):

time: 171 us -> 168 us (0.982)
  local copies, waits for them, and re-layouts: 4.59 us -> 1.35 us
    unnamed x5 -> x4, local copies, waits for them, and re-layouts: 4.59 us -> 1.35 us
    pallas_call x0 -> x1, Pallas kernels: none -> 1.86 us  [write(): pl.pallas_call(write_kernel, name='write', out_shape=tuple((pltpu.HBM(a.s...]
where the time goes in v5:
time: 168 us
  Pallas kernels  166 us (99%)
    pallas_call x1, Pallas kernels, bring(): pl.pallas_call(functools.partial(bring_kernel, nz, nx), name='bring', out...  79.7 us
    pallas_call x1, Pallas kernels, give(): pl.pallas_call(functools.partial(give_kernel, nz, nx), name='give', out_s...  67.7 us
    pallas_call x1, Pallas kernels, attend(): pl.pallas_call(attend_kernel, name='attend', out_shape=(pltpu.VMEM(lifted...  16.6 us

profile of v5, /device:TPU:1, one launch (start us, length us, event | category | flops | bytes accessed | tf_op | source)
XLA Modules:
  0.0 167.9 jit_solution(9711764535223179894)
XLA Ops:
  0.6 0.0 copy-start
  0.6 0.7 copy-done
  1.3 0.0 copy-start.1
  1.3 0.7 copy-done.1
  2.0 79.7 %bring.1 = (bf16[16,8,64,128]{3,2,1,0:T(8,128)(2,1)S(1)}, bf16[16,8,64,128]{3,2,1,0:T(8,128)(2,1)S(1)}, bf16[4,192,32,128]{3,2,1,0:T(8,128)(2,1)S(1)}, s32[16,8,...) custom-call(bf16[8,64,2048]{2,1,0:T(8,128)(2,1)} %q_ref.1, ...), custom_call_target="tpu_custom_call" | custom-call | tf_op jit(solution)/shard_map/bring/pallas_call | solution.py:249
  81.7 16.6 %attend.1 = (bf16[64,256,128]{2,1,0:T(8,128)(2,1)S(1)}, bf16[4,192,32,128]{3,2,1,0:T(8,128)(2,1)S(1)}, bf16[4,192,32,128]{3,2,1,0:T(8,128)(2,1)S(1)}) custom-call(s32[16,8,128]{2,1,0:T(8,128)S(1)} %get-tuple-element.16.i_ref, bf16[16,8,64,128]{3,2,1,0:T(8,128)(2,1)S(1)} %get-tuple-element.18.qh, ...), custom_call_target="tpu_custom_call", output_to_operand_aliasing={{0}: (4, {}), {2}: (3, {})} | custom-call | flops 1610612736 | bytes 4194304 | tf_op jit(solution)/shard_map/attend/pallas_call | solution.py:331
  98.4 67.7 %give.1 = (bf16[8,64,2048]{2,1,0:T(8,128)(2,1)S(1)}, bf16[6,32,2048]{2,1,0:T(8,128)(2,1)S(1)}, bf16[6,32,2048]{2,1,0:T(8,128)(2,1)S(1)}) custom-call(s32[16,8,128]{2,1,0:T(8,128)S(1)} %get-tuple-element.16.i_ref, bf16[4,192,32,128]{3,2,1,0:T(8,128)(2,1)} %get-tuple-element.17.ka_hbm, bf16[64,256,128]{2,1,0:T(8,128)(2,1)S(1)} %get-tuple-element.23.dscore_ref, ...), custom_call_target="tpu_custom_call" | custom-call | tf_op jit(solution)/shard_map/give/pallas_call | solution.py:528
  166.1 1.9 %write.1 = (bf16[8,64,2048]{2,1,0:T(8,128)(2,1)}, bf16[6,32,2048]{2,1,0:T(8,128)(2,1)}, bf16[6,32,2048]{2,1,0:T(8,128)(2,1)}) custom-call(bf16[8,64,2048]{2,1,0:T(8,128)(2,1)S(1)} %get-tuple-element.26.refs_0_, bf16[6,32,2048]{2,1,0:T(8,128)(2,1)S(1)} %get-tuple-element.27.refs_1_, bf16[6,32,2048]{2,1,0:T(8,128)(2,1)S(1)} %get-tuple-element.28.refs_2_), custom_call_target="tpu_custom_call" | custom-call | tf_op jit(solution)/shard_map/write/pallas_call | solution.py:563
Async XLA Ops:
  0.6 0.7 copy-start
  1.3 0.7 copy-start.1

commit v6 on v5

--- a/solution.py
+++ b/solution.py
@@ -101,7 +101,7 @@
     nz, nx,
     q_ref, g_ref, k_ref, v_ref, owner_ref, row_ref,
     qh, gh, va, ih, lifted_ref, inverse_ref, ka_hbm,
-    ka, i_ref, i_smem, s_in, r_in, s_y, r_y, s_c, r_c, own,
+    ka, i_ref, i_smem, o_vmem, w_vmem, s_in, r_in, s_y, r_y, s_c, r_c, own,
 ):
     y, z, x, c = place()
     chips = nz * nx
@@ -110,10 +110,18 @@
     quarter = k_ref.shape[1] // 4
     me = z * nx + x
     up, down, far = lax.rem(y + 1, 4), lax.rem(y + 3, 4), lax.rem(y + 2, 4)
+    lists = (
+        pltpu.make_async_copy(owner_ref, o_vmem, own.at[7]),
+        pltpu.make_async_copy(row_ref, w_vmem, own.at[8]),
+    )
+    for copy in lists:
+        copy.start()
     greet(nz, nx)
-
-    owners = owner_ref[...]
-    entries = (owners & 1) * part + (owners >> 1) * rows + row_ref[...]
+    for copy in lists:
+        copy.wait()
+
+    owners = o_vmem[...]
+    entries = (owners & 1) * part + (owners >> 1) * rows + w_vmem[...]
     i_ref[...] = jnp.zeros_like(i_ref)
     i_ref[: entries.shape[0], : entries.shape[1]] = entries
 
@@ -256,22 +264,24 @@
             pltpu.VMEM((pairs, 1, 2 * span_len), jnp.float32),
             pltpu.HBM(held.shape, bf16),
         ),
-        in_specs=[HBM] * 4 + [VMEM] * 2,
+        in_specs=[HBM] * 6,
         out_specs=(VMEM,) * 3 + (ANY,) + (VMEM,) * 2 + (HBM,),
         scratch_shapes=[
             pltpu.VMEM(held.shape, bf16),
             pltpu.VMEM(listed, jnp.int32),
             pltpu.SMEM((chips,) + listed, jnp.int32),
-            dma((5, chips)), dma((5, chips)), dma((2, 3)), dma((2, 3)), dma((2, 4)), dma((2, 4)), dma((7,)),
+            pltpu.VMEM((2, spans), jnp.int32),
+            pltpu.VMEM((2, spans), jnp.int32),
+            dma((5, chips)), dma((5, chips)), dma((2, 3)), dma((2, 3)), dma((2, 4)), dma((2, 4)), dma((9,)),
         ],
         compiler_params=pltpu.CompilerParams(
             collective_id=0, has_side_effects=True, vmem_limit_bytes=14 * MiB
         ),
-    )(*in_hbm(query, grad_out, keys, values), owner_list.T, row_list.T)
+    )(*in_hbm(query, grad_out, keys, values, owner_list.T, row_list.T))
 
 
 def attend_kernel(
-    i_ref, qh, gh, va, lifted_ref, inverse_ref, dscore_ref, dk_low, dv_low, dk, dv
+    i_hbm, qh, gh, va, lifted_ref, inverse_ref, dscore_ref, dk_low, dv_low, dk, dv, i_ref, sem
 ):
     quarters, rows, tok, _ = va.shape
     tokens = quarters * tok
@@ -297,10 +307,15 @@
         dscore_ref[p] = dscore
         return entries, contract(chance_low, grads, 1, 0)
 
+    lists = pltpu.make_async_copy(i_hbm, i_ref, sem)
+    lists.start()
+
     @pl.loop(0, rows)
     def _(r):
         dk[:, r] = jnp.zeros((quarters, tok, HD), jnp.float32)
         dv[:, r] = jnp.zeros((quarters, tok, HD), jnp.float32)
+
+    lists.wait()
 
     @pl.loop(0, pairs // unroll)
     def _(step):
@@ -332,9 +347,14 @@
         attend_kernel,
         name="attend",
         out_shape=(pltpu.VMEM(lifted.shape, jnp.bfloat16), held, held),
-        in_specs=[SMEM] + [VMEM] * 5,
+        in_specs=[ANY] + [VMEM] * 5,
         out_specs=(VMEM,) * 3,
-        scratch_shapes=[pltpu.VMEM(va.shape, jnp.float32)] * 2,
+        scratch_shapes=[
+            pltpu.VMEM(va.shape, jnp.float32),
+            pltpu.VMEM(va.shape, jnp.float32),
+            pltpu.SMEM(ih.shape, jnp.int32),
+            pltpu.SemaphoreType.DMA,
+        ],
         input_output_aliases={4: 0, 3: 2},
         compiler_params=pltpu.CompilerParams(vmem_limit_bytes=28 * MiB),
         cost_estimate=pl.CostEstimate(flops=3 * work, bytes_accessed=4 * MiB, transcendentals=0),
@@ -343,10 +363,10 @@
 
 def give_kernel(
     nz, nx,
-    i_ref, ka_hbm, dscore_ref, dk_ref, dv_ref,
+    i_hbm, ka_hbm, dscore_ref, dk_ref, dv_ref,
     gq, gk, gv,
-    ka, dq_ref, other, total, passed, arrived,
-    s_q, r_q, s_out, r_out, s_c, r_c, s_f, r_f, s_y, r_y, own_q, own_out, own_k,
+    i_ref, ka, dq_ref, other, total, passed, arrived,
+    s_q, r_q, s_out, r_out, s_c, r_c, s_f, r_f, s_y, r_y, own_q, own_out, own_k, own_i,
 ):
     y, z, x, c = place()
     chips = nz * nx
@@ -404,6 +424,8 @@
     query_own = pltpu.make_async_copy(dq_ref.at[me], gq.at[:, :, columns(me)], own_q)
     keys_in = pltpu.make_async_copy(ka_hbm, ka, own_k)
     keys_in.start()
+    lists = pltpu.make_async_copy(i_hbm, i_ref, own_i)
+    lists.start()
     pairs = dscore_ref.shape[0]
     per = dq_ref.shape[1]
     span_len = dq_ref.shape[2]
@@ -411,6 +433,7 @@
 
     def queries():
         keys_in.wait()
+        lists.wait()
 
         @pl.loop(0, pairs // unroll)
         def _(step):
@@ -529,9 +552,10 @@
         functools.partial(give_kernel, nz, nx),
         name="give",
         out_shape=(pltpu.VMEM((spans, span_len, chips * HD), bf16), row_out, row_out),
-        in_specs=[SMEM, HBM] + [VMEM] * 3,
+        in_specs=[ANY, HBM] + [VMEM] * 3,
         out_specs=(ANY,) * 3,
         scratch_shapes=[
+            pltpu.SMEM(ih.shape, jnp.int32),
             pltpu.VMEM(ka.shape, bf16),
             pltpu.VMEM((chips, spans, span_len, HD), bf16),
             pltpu.VMEM((4, 2) + piece, bf16),
@@ -540,7 +564,7 @@
             pltpu.VMEM((2, 2) + piece, bf16),
             dma((chips,)), dma((chips,)), dma((2, 2, chips)), dma((2, 2, chips)),
             dma((4, 2, nz, 2)), dma((4, 2, nz, 2)), dma((2, nz, 2)), dma((2, nz, 2)),
-            dma((2, 2, nz, 2)), dma((2, 2, nz, 2)), dma, dma((2, 2)), dma,
+            dma((2, 2, nz, 2)), dma((2, 2, nz, 2)), dma, dma((2, 2)), dma, dma,
         ],
         compiler_params=pltpu.CompilerParams(
             collective_id=1, has_side_effects=True, vmem_limit_bytes=32 * MiB

time: 168 us -> 164 us (0.976)
  Pallas kernels: 166 us -> 163 us
    pallas_call x1, Pallas kernels: 16.6 us -> 14.8 us  [attend(): pl.pallas_call(attend_kernel, name='attend', out_shape=(pltpu.VMEM(lifted...]
    pallas_call x1, Pallas kernels: 67.7 us -> 66 us  [give(): pl.pallas_call(functools.partial(give_kernel, nz, nx), name='give', out_s...]
where the time goes in v6:
time: 164 us
  Pallas kernels  163 us (99%)
    pallas_call x1, Pallas kernels, bring(): pl.pallas_call(functools.partial(bring_kernel, nz, nx), name='bring', out...  80.2 us
    pallas_call x1, Pallas kernels, give(): pl.pallas_call(functools.partial(give_kernel, nz, nx), name='give', out_s...  66 us
    pallas_call x1, Pallas kernels, attend(): pl.pallas_call(attend_kernel, name='attend', out_shape=(pltpu.VMEM(lifted...  14.8 us

profile of v6, /device:TPU:1, one launch (start us, length us, event | category | flops | bytes accessed | tf_op | source)
XLA Modules:
  0.0 163.6 jit_solution(11917990697820208718)
XLA Ops:
  0.6 80.2 %bring.1 = (bf16[16,8,64,128]{3,2,1,0:T(8,128)(2,1)S(1)}, bf16[16,8,64,128]{3,2,1,0:T(8,128)(2,1)S(1)}, bf16[4,192,32,128]{3,2,1,0:T(8,128)(2,1)S(1)}, s32[16,8,...) custom-call(bf16[8,64,2048]{2,1,0:T(8,128)(2,1)} %q_ref.1, ...), custom_call_target="tpu_custom_call" | custom-call | tf_op jit(solution)/shard_map/bring/pallas_call | solution.py:257
  80.9 14.8 %attend.1 = (bf16[64,256,128]{2,1,0:T(8,128)(2,1)S(1)}, bf16[4,192,32,128]{3,2,1,0:T(8,128)(2,1)S(1)}, bf16[4,192,32,128]{3,2,1,0:T(8,128)(2,1)S(1)}) custom-call(s32[16,8,128]{2,1,0:T(8,128)S(1)} %get-tuple-element.16.i_hbm, bf16[16,8,64,128]{3,2,1,0:T(8,128)(2,1)S(1)} %get-tuple-element.18.qh, ...), custom_call_target="tpu_custom_call", output_to_operand_aliasing={{0}: (4, {}), {2}: (3, {})} | custom-call | flops 1610612736 | bytes 4194304 | tf_op jit(solution)/shard_map/attend/pallas_call | solution.py:346
  95.7 66.0 %give.1 = (bf16[8,64,2048]{2,1,0:T(8,128)(2,1)S(1)}, bf16[6,32,2048]{2,1,0:T(8,128)(2,1)S(1)}, bf16[6,32,2048]{2,1,0:T(8,128)(2,1)S(1)}) custom-call(s32[16,8,128]{2,1,0:T(8,128)S(1)} %get-tuple-element.16.i_hbm, bf16[4,192,32,128]{3,2,1,0:T(8,128)(2,1)} %get-tuple-element.17.ka_hbm, bf16[64,256,128]{2,1,0:T(8,128)(2,1)S(1)} %get-tuple-element.23.dscore_ref, ...), custom_call_target="tpu_custom_call" | custom-call | tf_op jit(solution)/shard_map/give/pallas_call | solution.py:551
  161.7 1.9 %write.1 = (bf16[8,64,2048]{2,1,0:T(8,128)(2,1)}, bf16[6,32,2048]{2,1,0:T(8,128)(2,1)}, bf16[6,32,2048]{2,1,0:T(8,128)(2,1)}) custom-call(bf16[8,64,2048]{2,1,0:T(8,128)(2,1)S(1)} %get-tuple-element.26.refs_0_, bf16[6,32,2048]{2,1,0:T(8,128)(2,1)S(1)} %get-tuple-element.27.refs_1_, bf16[6,32,2048]{2,1,0:T(8,128)(2,1)S(1)} %get-tuple-element.28.refs_2_), custom_call_target="tpu_custom_call" | custom-call | tf_op jit(solution)/shard_map/write/pallas_call | solution.py:587

commit v7 on v6

--- a/solution.py
+++ b/solution.py
@@ -334,10 +334,12 @@
         for entries, key_terms in results:
             add(dk, entries, key_terms)
 
-    @pl.loop(0, rows)
+    @pl.loop(0, rows // 4)
     def _(r):
-        dk_low[:, r] = dk[:, r].astype(jnp.bfloat16)
-        dv_low[:, r] = dv[:, r].astype(jnp.bfloat16)
+        for u in range(4):
+            dk_low[:, 4 * r + u] = dk[:, 4 * r + u].astype(jnp.bfloat16)
+        for u in range(4):
+            dv_low[:, 4 * r + u] = dv[:, 4 * r + u].astype(jnp.bfloat16)
 
 
 def attend(ih, qh, gh, va, lifted, inverse):

time: 164 us -> 163 us (level)
  no operation moved by 1% of the time
where the time goes in v7:
time: 163 us
  Pallas kernels  162 us (99%)
    pallas_call x1, Pallas kernels, bring(): pl.pallas_call(functools.partial(bring_kernel, nz, nx), name='bring', out...  80.2 us
    pallas_call x1, Pallas kernels, give(): pl.pallas_call(functools.partial(give_kernel, nz, nx), name='give', out_s...  66 us
    pallas_call x1, Pallas kernels, attend(): pl.pallas_call(attend_kernel, name='attend', out_shape=(pltpu.VMEM(lifted...  14.4 us

profile of v7, /device:TPU:1, one launch (start us, length us, event | category | flops | bytes accessed | tf_op | source)
XLA Modules:
  0.0 163.1 jit_solution(2915605851547325132)
XLA Ops:
  0.6 80.2 %bring.1 = (bf16[16,8,64,128]{3,2,1,0:T(8,128)(2,1)S(1)}, bf16[16,8,64,128]{3,2,1,0:T(8,128)(2,1)S(1)}, bf16[4,192,32,128]{3,2,1,0:T(8,128)(2,1)S(1)}, s32[16,8,...) custom-call(bf16[8,64,2048]{2,1,0:T(8,128)(2,1)} %q_ref.1, ...), custom_call_target="tpu_custom_call" | custom-call | tf_op jit(solution)/shard_map/bring/pallas_call | solution.py:257
  80.9 14.4 %attend.1 = (bf16[64,256,128]{2,1,0:T(8,128)(2,1)S(1)}, bf16[4,192,32,128]{3,2,1,0:T(8,128)(2,1)S(1)}, bf16[4,192,32,128]{3,2,1,0:T(8,128)(2,1)S(1)}) custom-call(s32[16,8,128]{2,1,0:T(8,128)S(1)} %get-tuple-element.16.i_hbm, bf16[16,8,64,128]{3,2,1,0:T(8,128)(2,1)S(1)} %get-tuple-element.18.qh, ...), custom_call_target="tpu_custom_call", output_to_operand_aliasing={{0}: (4, {}), {2}: (3, {})} | custom-call | flops 1610612736 | bytes 4194304 | tf_op jit(solution)/shard_map/attend/pallas_call | solution.py:348
  95.2 66.0 %give.1 = (bf16[8,64,2048]{2,1,0:T(8,128)(2,1)S(1)}, bf16[6,32,2048]{2,1,0:T(8,128)(2,1)S(1)}, bf16[6,32,2048]{2,1,0:T(8,128)(2,1)S(1)}) custom-call(s32[16,8,128]{2,1,0:T(8,128)S(1)} %get-tuple-element.16.i_hbm, bf16[4,192,32,128]{3,2,1,0:T(8,128)(2,1)} %get-tuple-element.17.ka_hbm, bf16[64,256,128]{2,1,0:T(8,128)(2,1)S(1)} %get-tuple-element.23.dscore_ref, ...), custom_call_target="tpu_custom_call" | custom-call | tf_op jit(solution)/shard_map/give/pallas_call | solution.py:553
  161.2 1.9 %write.1 = (bf16[8,64,2048]{2,1,0:T(8,128)(2,1)}, bf16[6,32,2048]{2,1,0:T(8,128)(2,1)}, bf16[6,32,2048]{2,1,0:T(8,128)(2,1)}) custom-call(bf16[8,64,2048]{2,1,0:T(8,128)(2,1)S(1)} %get-tuple-element.26.refs_0_, bf16[6,32,2048]{2,1,0:T(8,128)(2,1)S(1)} %get-tuple-element.27.refs_1_, bf16[6,32,2048]{2,1,0:T(8,128)(2,1)S(1)} %get-tuple-element.28.refs_2_), custom_call_target="tpu_custom_call" | custom-call | tf_op jit(solution)/shard_map/write/pallas_call | solution.py:589

commit v8 on v7

--- a/solution.py
+++ b/solution.py
@@ -310,10 +310,10 @@
     lists = pltpu.make_async_copy(i_hbm, i_ref, sem)
     lists.start()
 
-    @pl.loop(0, rows)
+    @pl.loop(0, rows // 4)
     def _(r):
-        dk[:, r] = jnp.zeros((quarters, tok, HD), jnp.float32)
-        dv[:, r] = jnp.zeros((quarters, tok, HD), jnp.float32)
+        dk[:, pl.ds(4 * r, 4)] = jnp.zeros((quarters, 4, tok, HD), jnp.float32)
+        dv[:, pl.ds(4 * r, 4)] = jnp.zeros((quarters, 4, tok, HD), jnp.float32)
 
     lists.wait()
 

time: 163 us -> 163 us (level)
  no operation moved by 1% of the time
where the time goes in v8:
time: 163 us
  Pallas kernels  162 us (99%)
    pallas_call x1, Pallas kernels, bring(): pl.pallas_call(functools.partial(bring_kernel, nz, nx), name='bring', out...  80.2 us
    pallas_call x1, Pallas kernels, give(): pl.pallas_call(functools.partial(give_kernel, nz, nx), name='give', out_s...  66 us
    pallas_call x1, Pallas kernels, attend(): pl.pallas_call(attend_kernel, name='attend', out_shape=(pltpu.VMEM(lifted...  14.2 us

profile of v8, /device:TPU:1, one launch (start us, length us, event | category | flops | bytes accessed | tf_op | source)
XLA Modules:
  0.0 162.9 jit_solution(8546446829346104660)
XLA Ops:
  0.6 80.2 %bring.1 = (bf16[16,8,64,128]{3,2,1,0:T(8,128)(2,1)S(1)}, bf16[16,8,64,128]{3,2,1,0:T(8,128)(2,1)S(1)}, bf16[4,192,32,128]{3,2,1,0:T(8,128)(2,1)S(1)}, s32[16,8,...) custom-call(bf16[8,64,2048]{2,1,0:T(8,128)(2,1)} %q_ref.1, ...), custom_call_target="tpu_custom_call" | custom-call | tf_op jit(solution)/shard_map/bring/pallas_call | solution.py:257
  80.9 14.2 %attend.1 = (bf16[64,256,128]{2,1,0:T(8,128)(2,1)S(1)}, bf16[4,192,32,128]{3,2,1,0:T(8,128)(2,1)S(1)}, bf16[4,192,32,128]{3,2,1,0:T(8,128)(2,1)S(1)}) custom-call(s32[16,8,128]{2,1,0:T(8,128)S(1)} %get-tuple-element.16.i_hbm, bf16[16,8,64,128]{3,2,1,0:T(8,128)(2,1)S(1)} %get-tuple-element.18.qh, ...), custom_call_target="tpu_custom_call", output_to_operand_aliasing={{0}: (4, {}), {2}: (3, {})} | custom-call | flops 1610612736 | bytes 4194304 | tf_op jit(solution)/shard_map/attend/pallas_call | solution.py:348
  95.1 66.0 %give.1 = (bf16[8,64,2048]{2,1,0:T(8,128)(2,1)S(1)}, bf16[6,32,2048]{2,1,0:T(8,128)(2,1)S(1)}, bf16[6,32,2048]{2,1,0:T(8,128)(2,1)S(1)}) custom-call(s32[16,8,128]{2,1,0:T(8,128)S(1)} %get-tuple-element.16.i_hbm, bf16[4,192,32,128]{3,2,1,0:T(8,128)(2,1)} %get-tuple-element.17.ka_hbm, bf16[64,256,128]{2,1,0:T(8,128)(2,1)S(1)} %get-tuple-element.23.dscore_ref, ...), custom_call_target="tpu_custom_call" | custom-call | tf_op jit(solution)/shard_map/give/pallas_call | solution.py:553
  161.1 1.9 %write.1 = (bf16[8,64,2048]{2,1,0:T(8,128)(2,1)}, bf16[6,32,2048]{2,1,0:T(8,128)(2,1)}, bf16[6,32,2048]{2,1,0:T(8,128)(2,1)}) custom-call(bf16[8,64,2048]{2,1,0:T(8,128)(2,1)S(1)} %get-tuple-element.26.refs_0_, bf16[6,32,2048]{2,1,0:T(8,128)(2,1)S(1)} %get-tuple-element.27.refs_1_, bf16[6,32,2048]{2,1,0:T(8,128)(2,1)S(1)} %get-tuple-element.28.refs_2_), custom_call_target="tpu_custom_call" | custom-call | tf_op jit(solution)/shard_map/write/pallas_call | solution.py:589

commit v9 on v8

--- a/solution.py
+++ b/solution.py
@@ -211,7 +211,7 @@
 
     to_base2 = HD ** -0.5 * float(np.log2(np.e))
     pairs = lifted_ref.shape[0]
-    unroll = min(4, pairs)
+    unroll = min(8, pairs)
 
     def weigh(first, last):
         @pl.loop(first, last)

time: 163 us -> 163 us (level)
  no operation moved by 1% of the time
where the time goes in v9:
time: 163 us
  Pallas kernels  162 us (99%)
    pallas_call x1, Pallas kernels, bring(): pl.pallas_call(functools.partial(bring_kernel, nz, nx), name='bring', out...  79.2 us
    pallas_call x1, Pallas kernels, give(): pl.pallas_call(functools.partial(give_kernel, nz, nx), name='give', out_s...  66.9 us
    pallas_call x1, Pallas kernels, attend(): pl.pallas_call(attend_kernel, name='attend', out_shape=(pltpu.VMEM(lifted...  14.2 us

profile of v9, /device:TPU:1, one launch (start us, length us, event | category | flops | bytes accessed | tf_op | source)
XLA Modules:
  0.0 162.9 jit_solution(14490580425210113492)
XLA Ops:
  0.6 79.2 %bring.1 = (bf16[16,8,64,128]{3,2,1,0:T(8,128)(2,1)S(1)}, bf16[16,8,64,128]{3,2,1,0:T(8,128)(2,1)S(1)}, bf16[4,192,32,128]{3,2,1,0:T(8,128)(2,1)S(1)}, s32[16,8,...) custom-call(bf16[8,64,2048]{2,1,0:T(8,128)(2,1)} %q_ref.1, ...), custom_call_target="tpu_custom_call" | custom-call | tf_op jit(solution)/shard_map/bring/pallas_call | solution.py:257
  79.9 14.2 %attend.1 = (bf16[64,256,128]{2,1,0:T(8,128)(2,1)S(1)}, bf16[4,192,32,128]{3,2,1,0:T(8,128)(2,1)S(1)}, bf16[4,192,32,128]{3,2,1,0:T(8,128)(2,1)S(1)}) custom-call(s32[16,8,128]{2,1,0:T(8,128)S(1)} %get-tuple-element.16.i_hbm, bf16[16,8,64,128]{3,2,1,0:T(8,128)(2,1)S(1)} %get-tuple-element.18.qh, ...), custom_call_target="tpu_custom_call", output_to_operand_aliasing={{0}: (4, {}), {2}: (3, {})} | custom-call | flops 1610612736 | bytes 4194304 | tf_op jit(solution)/shard_map/attend/pallas_call | solution.py:348
  94.1 66.9 %give.1 = (bf16[8,64,2048]{2,1,0:T(8,128)(2,1)S(1)}, bf16[6,32,2048]{2,1,0:T(8,128)(2,1)S(1)}, bf16[6,32,2048]{2,1,0:T(8,128)(2,1)S(1)}) custom-call(s32[16,8,128]{2,1,0:T(8,128)S(1)} %get-tuple-element.16.i_hbm, bf16[4,192,32,128]{3,2,1,0:T(8,128)(2,1)} %get-tuple-element.17.ka_hbm, bf16[64,256,128]{2,1,0:T(8,128)(2,1)S(1)} %get-tuple-element.23.dscore_ref, ...), custom_call_target="tpu_custom_call" | custom-call | tf_op jit(solution)/shard_map/give/pallas_call | solution.py:553
  161.1 1.9 %write.1 = (bf16[8,64,2048]{2,1,0:T(8,128)(2,1)}, bf16[6,32,2048]{2,1,0:T(8,128)(2,1)}, bf16[6,32,2048]{2,1,0:T(8,128)(2,1)}) custom-call(bf16[8,64,2048]{2,1,0:T(8,128)(2,1)S(1)} %get-tuple-element.26.refs_0_, bf16[6,32,2048]{2,1,0:T(8,128)(2,1)S(1)} %get-tuple-element.27.refs_1_, bf16[6,32,2048]{2,1,0:T(8,128)(2,1)S(1)} %get-tuple-element.28.refs_2_), custom_call_target="tpu_custom_call" | custom-call | tf_op jit(solution)/shard_map/write/pallas_call | solution.py:589
